TPU v7x, 32 devices: a whole 2x2x4 slice. The times are simulated.
32 devices in a mesh: dp: 4 (over y, x), fsdp: 8 (over z, core).
Axes of the slice: x: 2, y: 2, z: 4, core: 2. Of those that a mesh axis runs over, the one named last changes fastest.
Arguments:
- tokens: bfloat16 [2, 32, 1024, 1024], P(None, ('dp', 'fsdp')), may hold values from -6 to 6
- document_length_list: int32 [2, 32, 8], P(None, ('dp', 'fsdp')), may hold values from 1 to 256, 1024 in all within a row
- joint_projection_weight: bfloat16 [1024, 3072], P('fsdp'), may hold values from -0.25 to 0.25
- attention_out_weight: bfloat16 [1024, 1024], P('fsdp'), may hold values from -0.375 to 0.375
- feed_up_weight: bfloat16 [1024, 4096], P('fsdp'), may hold values from -0.1875 to 0.1875
- feed_down_weight: bfloat16 [4096, 1024], P('fsdp'), may hold values from -0.09375 to 0.09375
- frozen_norm_gains: bfloat16 [2, 1024], P(None, 'fsdp'), may hold values from 0.5 to 1.5
- biases: bfloat16 [6, 1024], P(None, 'fsdp'), may hold values from -4 to 4
- hidden_up_bias: bfloat16 [4096], P('fsdp'), may hold values from -6 to 6
- query_down_adapter: bfloat16 [1024, 4], replicated, may hold values from -0.1875 to 0.1875
- query_up_adapter: bfloat16 [4, 1024], replicated, may hold values from -0.4375 to 0.4375
- value_down_adapter: bfloat16 [1024, 4], replicated, may hold values from -0.1875 to 0.1875
- value_up_adapter: bfloat16 [4, 1024], replicated, may hold values from -0.4375 to 0.4375
- cotangent: bfloat16 [2, 32, 1024, 1024], P(None, ('dp', 'fsdp')), may hold values from -6 to 6
Outputs:
- block_output: bfloat16 [2, 32, 1024, 1024], P(None, ('dp', 'fsdp'))
- input_grad: bfloat16 [2, 32, 1024, 1024], P(None, ('dp', 'fsdp'))
- grad_lora_a_q: float32 [1024, 4], replicated
- grad_lora_b_q: float32 [4, 1024], replicated
- grad_lora_a_v: float32 [1024, 4], replicated
- grad_lora_b_v: float32 [4, 1024], replicated
Inputs may be any that keep to these rules, and one draw needn't show every extreme that they name: `document_length_list`: the 8 lengths of a slot sum to 1024, and the largest of them is exactly 256.
All inputs are finite; a program needn't handle non-finite values.
Results may differ from a plain program's by a relative error of at most 0.015.
Values may be sent and summed in bfloat16 or wider, within the bound.
No kernel may reach another device: no remote copies, remote signals or barrier semaphores. Data moves between devices by JAX's collectives and lax.ppermute only.
A program may use at most 320 MiB of HBM per device.

v0:
```python
import functools
import math

import jax
import jax.numpy as jnp
from jax import lax
from jax.experimental import pallas as pl
from jax.experimental.pallas import tpu as pltpu
from jax.sharding import PartitionSpec as P

f32 = jnp.float32
bf16 = jnp.bfloat16
LANES = 128
PAIR = 128
BAND = 3
EPS = 1e-5
MASKED = -1e30
SCORE_SCALE = 0.125 * math.log2(math.e)
GELU_C = math.sqrt(2.0 / math.pi)
VMEM_LIMIT = 58 * 2**20
COST = 8
NT = (((1,), (1,)), ((), ()))
TN = (((0,), (0,)), ((), ()))


def dot(a, b):
    return jnp.dot(a, b, preferred_element_type=f32)


def dot_nt(a, b):
    return lax.dot_general(a, b, NT, preferred_element_type=f32)


def dot_tn(a, b):
    return lax.dot_general(a, b, TN, preferred_element_type=f32)


def params():
    return pltpu.CompilerParams(vmem_limit_bytes=VMEM_LIMIT)


def resident(array):
    zeros = (0,) * array.ndim
    return pl.BlockSpec(array.shape, lambda *_: zeros, pipeline_mode=pl.Buffered(1))


def normalise(x):
    centred = x - jnp.mean(x, axis=-1, keepdims=True)
    r = lax.rsqrt(jnp.mean(centred * centred, axis=-1, keepdims=True) + EPS)
    return centred * r, r


def norm_back(n, r, w):
    return r * (w - jnp.mean(w, axis=-1, keepdims=True) - n * jnp.mean(w * n, axis=-1, keepdims=True))


def gelu_and_slope(x):
    x2 = x * x
    t = jnp.tanh(x * (GELU_C + (GELU_C * 0.044715) * x2))
    half = 0.5 + 0.5 * t
    act = x * half
    slope = half + (act * (1.0 - half)) * (2 * GELU_C + (6 * GELU_C * 0.044715) * x2)
    return act, slope


def ring_pairs(dp, fsdp, move):
    pairs = []
    for d in range(dp):
        for f in range(fsdp):
            e, g = move(d, f)
            pairs.append((d * fsdp + f, e * fsdp + g))
    return pairs


def after(x, others):
    return lax.optimization_barrier((x, others))[0]


def after_all(xs, others):
    return lax.optimization_barrier((xs, others))[0]


class Gather:
    def __init__(self, dp, fsdp):
        self.dp, self.fsdp = dp, fsdp

    def move(self, x, where):
        return lax.ppermute(x, ("dp", "fsdp"), ring_pairs(self.dp, self.fsdp, where))

    def step_1(self, mine):
        fsdp = self.fsdp
        return [self.move(mine, lambda d, f, k=k: (d, (f + 2 * k) % fsdp)) for k in range(1, fsdp // 2)]

    def all_far(self, near):
        near = [jnp.broadcast_to(x[None], (self.dp,) + x.shape) for x in near]
        return lax.all_to_all(jnp.concatenate(near, axis=1), "dp", 0, 0, tiled=False)

    def each_far(self, near):
        near = stack(near) if len(near) > 1 else near[0]
        return [near] + [self.move(near, lambda d, f, e=e: (d ^ e, f)) for e in range(1, self.dp)]

    def swap(self, x):
        return self.move(x, lambda d, f: (d, f ^ 1))


def pieces(shard, other_shard, far, other_far, shard_column=0, far_column=0):
    made = [(shard, shard_column, 0, "shard"), (other_shard, shard_column, 1, "shard")]
    for swapped, arrays in ((0, far), (1, other_far)):
        if len(arrays) == 1:
            made.append((arrays[0], far_column, swapped, "all"))
        else:
            made += [(x, far_column, swapped, e) for e, x in enumerate(arrays)]
    return made


def copies(weight, refs, whole, sems, place, cols, base, dp, fsdp):
    made = []
    start, size = cols
    rows = whole.shape[0] // fsdp
    part = rows // dp
    index = place[1]

    def add(source, first, at, rows):
        target = whole.at[pl.ds(at, rows), pl.ds(start - base, size)]
        made.append(pltpu.make_async_copy(source.at[:, pl.ds(first + start, size)], target, sems.at[len(made)]))

    for (_, column, swapped, what), ref in zip(weight, refs):
        other = swapped * (1 - 2 * lax.rem(index, 2))
        if what == "whole":
            add(ref, column, 0, whole.shape[0])
        elif what == "shard":
            add(ref, column, pl.multiple_of((index + other) * rows, rows), rows)
        else:
            for e in range(dp) if what == "all" else [what]:
                quarter = e if what == "all" else jnp.bitwise_xor(place[0], e)
                for k in range(1, fsdp // 2):
                    owner = lax.rem(index + fsdp - 2 * k, fsdp) + other
                    at = pl.multiple_of(owner * rows + quarter * part, part)
                    here = pl.ds((k - 1) * part, part)
                    add(ref.at[e, here] if what == "all" else ref.at[here], column, at, part)
    return made


def copy_count(weight, dp, fsdp):
    count = 0
    for _, _, _, what in weight:
        count += 1 if what in ("whole", "shard") else (fsdp // 2 - 1) * (dp if what == "all" else 1)
    return count


def weight_call(kernel, name, weights, order, grid, blocked, in_specs, out_specs, out_shape, scratch, cost, fsdp, old=()):
    dp = lax.axis_size("dp")
    arrays = [[piece[0] for piece in w] for w, _ in weights]
    flat = [a for some in arrays for a in some]
    counts = [copy_count(weights[i][0], dp, fsdp) for i, _, _ in order]

    def body(*refs):
        refs = list(refs)
        place = [lax.axis_index("dp"), lax.axis_index("fsdp")]
        take = lambda n: [refs.pop(0) for _ in range(n)]
        sources = [take(len(some)) for some in arrays]
        ins, _, outs = take(len(blocked)), take(len(old)), take(len(out_shape))
        wholes, sems = take(len(weights)), take(len(order))

        first_step = pl.program_id(0) == 0
        for axis in range(1, len(grid)):
            first_step = first_step & (pl.program_id(axis) == 0)

        def group(n):
            i, start, size = order[n]
            base = start if wholes[i].shape[1] == size else 0
            return copies(weights[i][0], sources[i], wholes[i], sems[n], place, (start, size), base, dp, fsdp)

        @pl.when(first_step)
        def _():
            for n in range(len(order)):
                for copy in group(n):
                    copy.start()

        def wait(n):
            @pl.when(first_step)
            def _():
                for copy in group(n):
                    copy.wait()

        kernel(wholes, wait, ins, outs, refs)

    return pl.pallas_call(
        body,
        grid=grid,
        in_specs=[pl.BlockSpec(memory_space=pltpu.HBM)] * len(flat)
        + in_specs
        + [pl.BlockSpec(memory_space=pl.ANY)] * len(old),
        out_specs=out_specs,
        scratch_shapes=[pltpu.VMEM(shape, bf16) for _, shape in weights]
        + [pltpu.SemaphoreType.DMA((n,)) for n in counts]
        + scratch,
        out_shape=out_shape,
        compiler_params=params(),
        cost_estimate=pl.CostEstimate(flops=cost // COST, bytes_accessed=2**20, transcendentals=0),
        input_output_aliases={len(flat) + len(blocked) + i: i for i in range(len(old))},
        name=name,
    )(*flat, *blocked, *old)


def own_quarter(rows):
    return pl.ds(pl.multiple_of(lax.axis_index("dp") * rows, rows), rows)


def stack_rows(arrays, rows):
    arrays = [a.astype(f32) for a in arrays]
    used = sum(a.shape[0] for a in arrays)
    return jnp.concatenate(arrays + [jnp.zeros((rows - used, arrays[0].shape[1]), f32)], axis=0).astype(bf16)


def stack_kernel(*refs):
    rows = refs[0].shape[0]
    for i, ref in enumerate(refs[:-1]):
        refs[-1][i * rows : (i + 1) * rows, :] = ref[...]


def stack(arrays):
    rows, columns = arrays[0].shape
    return local_call(stack_kernel, "stack", [(rows * len(arrays), columns)], arrays)[0]


def cut_kernel(joint, biases, gains, hidden, first, part):
    half = joint.shape[1] // 6
    for i in range(3):
        first[:, i * half : (i + 1) * half] = joint[:, 2 * i * half : (2 * i + 1) * half]
    small = [biases[...], gains[...], hidden[...].astype(f32).reshape(-1, LANES)]
    first[:, 3 * half :] = stack_rows(small, first.shape[0])
    part[...] = first[own_quarter(part.shape[0]), :]


def local_call(kernel, name, shapes, arrays):
    return pl.pallas_call(
        kernel,
        out_shape=[jax.ShapeDtypeStruct(s, bf16) for s in shapes],
        compiler_params=params(),
        name=name,
    )(*arrays)


def cut(joint, biases, gains, hidden, dp):
    rows, width = joint.shape
    columns = width // 2 + LANES
    return local_call(cut_kernel, "cut", [(rows, columns), (rows // dp, columns)], [joint, biases, gains, hidden])


def pack_kernel(chunks, shards, joint, up, down, wo, q_down, q_up, v_down, v_up, *refs):
    outs, parts = refs[:2], refs[2:4]
    down_map, up_map = refs[4:]
    hidden, width = down.shape
    part = hidden // chunks
    half = joint.shape[1] // 6
    for i in range(3):
        outs[0][:, i * half : (i + 1) * half] = joint[:, (2 * i + 1) * half : (2 * i + 2) * half]
    for j in range(chunks):
        out, at = (outs[1], (j - 1) * 2 * width) if j else (outs[0], 3 * half)
        for s in range(shards):
            start = s * hidden + j * part
            out[:, at + s * part : at + (s + 1) * part] = up[:, start : start + part]
        out[:, at + width : at + 2 * width] = down[j * part : (j + 1) * part, :]
    outs[0][:, 3 * half + 2 * width :] = wo[...]
    for out, part_ref in zip(outs, parts):
        part_ref[...] = out[own_quarter(part_ref.shape[0]), :]
    rank = q_up.shape[0]
    down_map[...] = jnp.zeros_like(down_map)
    down_map[:, :rank] = q_down[...]
    down_map[:, rank : 2 * rank] = v_down[...]
    zero = jnp.zeros(q_up.shape, f32)
    rows = [jnp.concatenate([q_up[...].astype(f32) * 8.0, zero], axis=1)]
    rows += [jnp.concatenate([zero, v_up[...].astype(f32) * 8.0], axis=1)]
    up_map[...] = stack_rows(rows, up_map.shape[0])


def pack(joint, up, down, wo, adapters, chunks, shards, dp):
    rows, width = up.shape[0], down.shape[1]
    shapes = [(rows, joint.shape[1] // 2 + 3 * width), (rows, 2 * (chunks - 1) * width)]
    shapes += [(r // dp, c) for r, c in shapes]
    shapes += [(width, LANES), (LANES, 2 * width)]
    return local_call(functools.partial(pack_kernel, chunks, shards), "pack", shapes, [joint, up, down, wo, *adapters])


def project_slot(first, carried, shards, w, wait, ins, outs, load):
    rows_in, down, up = ins[:3]
    q_ref, k_ref, v_ref = outs[:3]
    half = q_ref.shape[1]
    width = 2 * half
    cols = slice(0, half) if first else slice(half, width)
    wait(0)
    if first:
        low_ref, normed_ref, vec = outs[3:6]

        @pl.when(pl.program_id(0) == 0)
        def _():
            if carried:
                rows = w.shape[0] // shards
                parts = [w[s * rows : s * rows + vec.shape[0], 3 * half :] for s in range(shards)]
                vec[...] = jnp.concatenate(parts, axis=1).astype(f32)
            else:
                vec[...] = ins[3][...]
    else:
        low_in, vec = ins[3:]
    load.wait()
    sub = 256
    state = {}

    def norm(r):
        rr = slice(r, r + sub)
        if first:
            n, _ = normalise(rows_in[rr, :].astype(f32))
            normed = (n * vec[6:7, :] + vec[0:1, :]).astype(bf16)
            normed_ref[rr, :] = normed
        else:
            normed = rows_in[rr, :]
        state[r] = normed

    def mix(r):
        rr = slice(r, r + sub)
        normed = state.pop(r)
        k_ref[rr, :] = dot(normed, w[:, half : 2 * half]).astype(bf16)
        if first:
            low = dot(normed, down[...]).astype(bf16)
            low_ref[rr, :] = low
        else:
            low = low_in[rr, :]
        q = dot(normed, w[:, :half]) + dot(low, up[:, cols]) + vec[2:3, cols]
        q_ref[rr, :] = (q * SCORE_SCALE).astype(bf16)
        v = dot(normed, w[:, 2 * half : 3 * half]) + dot(low, up[:, width:][:, cols]) + vec[3:4, cols]
        v_ref[rr, :] = v.astype(bf16)

    pipelined(list(range(0, rows_in.shape[0], sub)), (norm, mix), (0, 1))


def heads_kernel(first, carried, shards, pairs, wholes, wait, ins, outs, scratch):
    lengths, x_hbm, ins = ins[0], ins[1], ins[2:]
    mask, x_ref, q_ref, k_ref, v_ref, *normed_ref, sems = scratch
    o_ref, p_ref, linv_ref = outs[-3:]
    seq, half = q_ref.shape
    blocks = seq // LANES
    slot, step = pl.program_id(0), pl.program_id(1)

    def rows(s):
        return pl.ds(pl.multiple_of(s * seq, seq), seq)

    def load(s):
        return pltpu.make_async_copy(x_hbm.at[rows(s)], x_ref, sems.at[0])

    cols = pl.ds(0 if first else half, half)
    stores = [(ref, out.at[rows(slot), cols]) for ref, out in zip((q_ref, k_ref, v_ref), outs)]
    if first:
        stores.append((normed_ref[0], outs[4].at[rows(slot)]))
    stores = [pltpu.make_async_copy(a, b, sems.at[1 + i]) for i, (a, b) in enumerate(stores)]

    @pl.when((slot == 0) & (step == 0))
    def _():
        load(0).start()

    @pl.when(step == 0)
    def _():
        own = [q_ref, k_ref, v_ref] + ([outs[3], normed_ref[0], outs[5]] if first else [])
        project_slot(first, carried, shards, wholes[0], wait, [x_ref] + list(ins), own, load(slot))
        for store in stores:
            store.start()
        fill_masks(lengths, slot, mask, blocks)

    @pl.when((step == 1) & (slot + 1 < pl.num_programs(0)))
    def _():
        load(slot + 1).start()

    @pl.when(step != 0)
    def _():
        at = pl.multiple_of((step - 1) * pairs * PAIR, pairs * PAIR)
        attend_pairs(pairs, blocks, at, q_ref, k_ref, v_ref, o_ref, p_ref, linv_ref, mask)

    @pl.when(step == pl.num_programs(1) - 1)
    def _():
        for store in stores:
            store.wait()


def heads(weight, fsdp, lengths, x, down, up, vec=None, low=None, old=()):
    tokens, width = x.shape
    slots = lengths.shape[0]
    seq = tokens // slots
    blocks, heads2, pairs = seq // LANES, width // PAIR, 2
    steps = heads2 // pairs // 2
    first = low is None
    here = 0 if first else 1
    far = pl.BlockSpec(memory_space=pltpu.HBM)
    thin = pl.BlockSpec((seq, LANES), lambda s, j: (s, 0))
    group = lambda j: here * steps + jnp.maximum(j - 1, 0)
    tile = pl.BlockSpec((seq, pairs * PAIR), lambda s, j: (s, group(j)))
    probs = (pairs, blocks, BAND * LANES, 2 * LANES)
    sums = (pairs, blocks, 2 * LANES)
    ins = [lengths, x, down, up]
    in_specs = [pl.BlockSpec(memory_space=pltpu.SMEM), far, resident(down), resident(up)]
    outs, out_specs = [jax.ShapeDtypeStruct((tokens, width), bf16)] * 3, [far] * 3
    if first:
        outs = outs + [jax.ShapeDtypeStruct((tokens, n), bf16) for n in (LANES, width)]
        outs = outs + [jax.ShapeDtypeStruct((16, width), f32)]
        out_specs = out_specs + [thin, far, pl.BlockSpec((16, width), lambda s, j: (0, 0))]
    else:
        ins, in_specs = ins + [low], in_specs + [thin]
    if vec is not None:
        ins, in_specs = ins + [vec], in_specs + [resident(vec)]
    outs = outs + [
        jax.ShapeDtypeStruct((tokens, width), bf16),
        jax.ShapeDtypeStruct((slots, heads2) + probs[1:], bf16),
        jax.ShapeDtypeStruct((slots, heads2) + sums[1:], f32),
    ]
    out_specs = out_specs + [
        tile,
        pl.BlockSpec((1,) + probs, lambda s, j: (s, group(j), 0, 0, 0)),
        pl.BlockSpec((1,) + sums, lambda s, j: (s, group(j), 0, 0)),
    ]
    carried = first and vec is None
    columns = 3 * width // 2 + (LANES if carried else 0)
    return weight_call(
        functools.partial(heads_kernel, first, carried, fsdp, pairs),
        "heads",
        [(weight, (width, columns))],
        [(0, 0, columns)],
        (slots, 1 + steps),
        ins,
        in_specs,
        out_specs,
        outs,
        [pltpu.VMEM((blocks, BAND * LANES, LANES), f32), pltpu.VMEM((seq, width), bf16)]
        + [pltpu.VMEM((seq, width // 2), bf16)] * 3
        + [pltpu.VMEM((seq, width), bf16)] * first
        + [pltpu.SemaphoreType.DMA((5,))],
        9 * tokens * width * width,
        fsdp,
        old,
    )


def fill_masks(lengths, slot, mask, blocks):
    starts = []
    total = jnp.int32(0)
    for d in range(lengths.shape[1]):
        starts.append(total)
        total = total + lengths[slot, d]
    for qb in range(blocks):
        first = max(0, qb - BAND + 1)
        rows = (qb - first + 1) * LANES
        query = qb * LANES + lax.broadcasted_iota(jnp.int32, (8, LANES), 1)
        begin = jnp.zeros((8, LANES), jnp.int32)
        for start in starts:
            begin = jnp.where(query >= start, start, begin)
        key = first * LANES + lax.broadcasted_iota(jnp.int32, (rows, LANES), 0)
        ok = (key >= begin[0:1]) & (key <= query[0:1])
        mask[qb, :rows, :] = jnp.where(ok, 0.0, MASKED)


def half_lanes():
    return lax.broadcasted_iota(jnp.int32, (LANES, LANES), 1) < 64


def half_rows():
    return lax.broadcasted_iota(jnp.int32, (LANES, LANES), 0) < 64


def split_heads(x, left):
    zero = jnp.zeros_like(x)
    return jnp.concatenate([jnp.where(left, x, zero), jnp.where(left, zero, x)], axis=0)


def pipelined(units, stages, lags):
    for t in range(len(units) + lags[-1]):
        for stage, lag in zip(stages, lags):
            if 0 <= t - lag < len(units):
                stage(units[t - lag])


def geometry(qb):
    first = max(0, qb - BAND + 1)
    return first * LANES, (qb - first + 1) * LANES


def attend_pairs(pairs, blocks, at, q_ref, k_ref, v_ref, o_ref, p_ref, linv_ref, mask):
    left, top = half_lanes(), half_rows()
    scores, probs = {}, {}

    def score(unit):
        pair, qb = unit
        cols = pl.ds(at + pair * PAIR, PAIR)
        key0, rows = geometry(qb)
        q = split_heads(q_ref[qb * LANES : (qb + 1) * LANES, cols], left)
        scores[unit] = dot_nt(k_ref[key0 : key0 + rows, cols], q)

    def soften(unit):
        pair, qb = unit
        key0, rows = geometry(qb)
        bias = mask[qb, :rows, :]
        s = scores.pop(unit) + jnp.concatenate([bias, bias], axis=1)
        p = jnp.exp2(s - jnp.max(s, axis=0, keepdims=True))
        linv = 1.0 / jnp.sum(p, axis=0, keepdims=True)
        linv_ref[0, pair, qb : qb + 1, :] = linv
        low = p.astype(bf16)
        p_ref[0, pair, qb, :rows, :] = low
        probs[unit] = (low, linv)

    def mix(unit):
        pair, qb = unit
        key0, rows = geometry(qb)
        low, linv = probs.pop(unit)
        o = dot_tn(v_ref[key0 : key0 + rows, pl.ds(at + pair * PAIR, PAIR)], low)
        o = jnp.where(top, o[:, :LANES] * linv[:, :LANES], o[:, LANES:] * linv[:, LANES:])
        o_ref[qb * LANES : (qb + 1) * LANES, pair * PAIR : (pair + 1) * PAIR] = o.T.astype(bf16)

    units = [(pair, qb) for qb in range(blocks) for pair in range(pairs)]
    pipelined(units, (score, soften, mix), (0, 2, 5))


def attend_back_kernel(
    pairs, blocks, q_ref, k_ref, v_ref, g_ref, o_ref, p_ref, linv_ref, low, normed, up, *refs
):
    dq_ref, dk_ref, dv_ref, glow_ref, grads, dk_sum, dv_sum, glow_sum = refs
    left, top = half_lanes(), half_rows()
    ones = jnp.ones((BAND * LANES, LANES), bf16)
    dk_sum[...] = jnp.zeros_like(dk_sum)
    dv_sum[...] = jnp.zeros_like(dv_sum)
    first, second = {}, {}

    def grad_probs(unit):
        pair, qb = unit
        cols = slice(pair * PAIR, (pair + 1) * PAIR)
        key0, rows = geometry(qb)
        here = slice(qb * LANES, (qb + 1) * LANES)
        linv = linv_ref[0, pair, qb : qb + 1, :]
        linv = jnp.where(top, linv[:, :LANES], linv[:, LANES:]).T
        g = g_ref[here, cols].astype(f32) * linv
        delta = split_heads(-(g * o_ref[here, cols].astype(f32)).astype(bf16), left)
        g = split_heads(g.astype(bf16), left)
        values = jnp.concatenate([v_ref[key0 : key0 + rows, cols], ones[:rows]], axis=1)
        first[unit] = (dot_nt(values, jnp.concatenate([g, delta], axis=1)), g)

    def grad_values(unit):
        pair, qb = unit
        cols = slice(pair * PAIR, (pair + 1) * PAIR)
        key0, rows = geometry(qb)
        dp, g = first.pop(unit)
        low = p_ref[0, pair, qb, :rows, :]
        second[unit] = low * dp.astype(bf16)
        dv_sum[key0 : key0 + rows, cols] += dot(low, g)

    def grad_queries_keys(unit):
        pair, qb = unit
        cols = slice(pair * PAIR, (pair + 1) * PAIR)
        key0, rows = geometry(qb)
        here = slice(qb * LANES, (qb + 1) * LANES)
        ds = second.pop(unit)
        dk_sum[key0 : key0 + rows, cols] += dot(ds, split_heads(q_ref[here, cols], left))
        dq = dot_tn(k_ref[key0 : key0 + rows, cols], ds)
        dq = jnp.where(top, dq[:, :LANES], dq[:, LANES:]) * 0.125
        dq_ref[here, cols] = dq.T.astype(bf16)

    units = [(pair, qb) for qb in range(blocks) for pair in range(pairs)]
    pipelined(units, (grad_probs, grad_values, grad_queries_keys), (0, 2, 4))
    dk_ref[...] = (dk_sum[...] * (0.125 / SCORE_SCALE)).astype(bf16)
    dv_ref[...] = dv_sum[...].astype(bf16)

    slot, step, last = pl.program_id(0), pl.program_id(1), pl.num_programs(1) - 1
    width = normed.shape[1]
    at = pl.multiple_of(step * pairs * PAIR, pairs * PAIR)
    here = pl.ds(at, pairs * PAIR)
    both = jnp.concatenate([dq_ref[...], dv_ref[...]], axis=1)
    part = dot_tn(low[...], both)
    part = jnp.concatenate([part[0:4, : pairs * PAIR], part[4:8, pairs * PAIR :]], axis=0) * 8.0
    grads[0:8, here] = jnp.where(slot == 0, part, grads[0:8, here] + part)
    glow = dot_nt(both, jnp.concatenate([up[:, here], up[:, pl.ds(width + at, pairs * PAIR)]], axis=1))
    glow_sum[...] = jnp.where(step == 0, glow, glow_sum[...] + glow)

    @pl.when(step == last)
    def _():
        glow = glow_sum[...].astype(bf16)
        glow_ref[...] = glow
        part = dot_tn(glow, normed[...])[0:8]
        grads[8:16, :] = jnp.where(slot == 0, part, grads[8:16, :] + part)


def attend_back(slots, q, k, v, g, o, p, linv, low, normed, up):
    tokens, width = q.shape
    seq = tokens // slots
    blocks, heads2, pairs = seq // LANES, width // PAIR, 2
    rows = BAND * LANES
    tile = pl.BlockSpec((seq, pairs * PAIR), lambda s, h: (s, h))
    thin = pl.BlockSpec((seq, LANES), lambda s, h: (s, 0))
    return pl.pallas_call(
        functools.partial(attend_back_kernel, pairs, blocks),
        grid=(slots, heads2 // pairs),
        in_specs=[tile] * 5
        + [
            pl.BlockSpec((1, pairs, blocks, rows, 2 * LANES), lambda s, h: (s, h, 0, 0, 0)),
            pl.BlockSpec((1, pairs, blocks, 2 * LANES), lambda s, h: (s, h, 0, 0)),
            thin,
            pl.BlockSpec((seq, width), lambda s, h: (s, 0)),
            resident(up),
        ],
        out_specs=[tile] * 3 + [thin, pl.BlockSpec((16, width), lambda s, h: (0, 0))],
        scratch_shapes=[pltpu.VMEM((seq, pairs * PAIR), f32)] * 2 + [pltpu.VMEM((seq, LANES), f32)],
        out_shape=[jax.ShapeDtypeStruct(q.shape, bf16)] * 3
        + [jax.ShapeDtypeStruct((tokens, LANES), bf16), jax.ShapeDtypeStruct((16, width), f32)],
        compiler_params=params(),
        cost_estimate=pl.CostEstimate(flops=14 * tokens * width * width // COST, bytes_accessed=2**20, transcendentals=0),
        name="attend_back",
    )(q, k, v, g, o, p, linv, low, normed, up)


def feed_chunk(wait, first, normed, cot, w, at, bias):
    width = cot.shape[1]
    wait(first)
    wait(first + 1)
    size = width // 4
    up, down = slice(at, at + width), slice(at + width, at + 2 * width)
    acts, grads = [], []
    for i in range(0, width, size):
        grad = dot_nt(cot, w[i : i + size, down])
        act, slope = gelu_and_slope(dot(normed, w[:, at + i : at + i + size]) + bias[:, i : i + size])
        acts.append(act.astype(bf16))
        grads.append((slope * grad).astype(bf16))
    return dot(jnp.concatenate(acts, axis=1), w[:, down]), dot_nt(jnp.concatenate(grads, axis=1), w[:, up])


def feed_first_kernel(wholes, wait, ins, outs, _):
    tok, att, cot, vec = ins
    h1_ref, normed_ref, o_ref, g_ref = outs
    width = tok.shape[1]
    wait(0)
    h1 = tok[...].astype(f32) + dot(att[...], wholes[0][:, 2 * width :]) + vec[4:5, :]
    h1_ref[...] = h1
    n, _ = normalise(h1)
    normed = (n * vec[7:8, :] + vec[1:2, :]).astype(bf16)
    normed_ref[...] = normed
    o_ref[...], g_ref[...] = feed_chunk(wait, 1, normed, cot[...], wholes[0], 0, vec[8:9, :])


def feed_last_kernel(wholes, wait, ins, outs, scratch):
    normed, cot, vec, h1, old_o, old_g = ins
    out_ref, gh_ref, ga_ref = outs
    x_ref, o_sum, g_sum, sems = scratch
    rows, width = cot.shape
    here = pl.ds(pl.multiple_of(pl.program_id(0) * rows, rows), rows)
    loads = [(old_o, o_sum), (old_g, g_sum), (h1, x_ref)]
    loads = [pltpu.make_async_copy(a.at[here], b, sems.at[i]) for i, (a, b) in enumerate(loads)]
    for load in loads:
        load.start()
    chunks = wholes[0].shape[1] // (2 * width)
    for j in range(chunks):
        bias = vec[9 + j : 10 + j, :]
        o, g = feed_chunk(wait, 2 * j, normed[...], cot[...], wholes[0], 2 * j * width, bias)
        if j == 0:
            for load in loads:
                load.wait()
        if j < chunks - 1:
            o_sum[...] += o
            g_sum[...] += g
    x = x_ref[...]
    out_ref[...] = (x + (o_sum[...] + o) + vec[5:6, :]).astype(bf16)
    n, r = normalise(x)
    grad = cot[...].astype(f32) + norm_back(n, r, (g_sum[...] + g) * vec[7:8, :])
    low = grad.astype(bf16)
    gh_ref[...] = low
    wait(2 * chunks)
    ga_ref[...] = dot_nt(low, wholes[1][...]).astype(bf16)


def feed_call(kernel, name, weights, order, fsdp, rowwise, vec, far, out_types):
    tokens, width = rowwise[0].shape
    rows = 512
    row = pl.BlockSpec((rows, width), lambda i: (i, 0))
    scratch = [pltpu.VMEM((rows, width), f32)] * len(far)
    return weight_call(
        kernel,
        name,
        weights,
        order,
        (tokens // rows,),
        rowwise + [vec] + far,
        [row] * len(rowwise) + [resident(vec)] + [pl.BlockSpec(memory_space=pltpu.HBM)] * len(far),
        [row] * len(out_types),
        [jax.ShapeDtypeStruct((tokens, width), t) for t in out_types],
        scratch + ([pltpu.SemaphoreType.DMA((len(far),))] if far else []),
        18 * tokens * width * width,
        fsdp,
    )


def feed_order(width, chunks):
    return [(0, (2 * j + 1 - i) * width, width) for j in range(chunks) for i in (0, 1)]


def feed_first(feeds, fsdp, tok, att, cot, vec):
    width = tok.shape[1]
    weights = [(feeds[0], (width, 3 * width))]
    order = [(0, 2 * width, width)] + feed_order(width, 1)
    types = [f32, bf16, f32, f32]
    return feed_call(feed_first_kernel, "feed_first", weights, order, fsdp, [tok, att, cot], vec, [], types)


def feed_last(feeds, fsdp, h1, normed, o, g, cot, vec):
    width = cot.shape[1]
    weights = [(feeds[1], (width, 6 * width)), (feeds[0], (width, width))]
    order = feed_order(width, 3) + [(1, 2 * width, width)]
    rowwise, far = [normed, cot], [h1, o, g]
    return feed_call(feed_last_kernel, "feed_last", weights, order, fsdp, rowwise, vec, far, [bf16] * 3)


def input_kernel(wholes, wait, ins, outs, _):
    dq, dk, dv, glow, down, vec, tok, gh = ins
    (out_ref,) = outs
    half = dq.shape[1] // 2
    g = dot_nt(glow[...], down[...])
    for i, w in enumerate(wholes):
        wait(i)
        cols = slice(i * half, (i + 1) * half)
        g = g + dot_nt(dq[:, cols], w[:, :half])
        g = g + dot_nt(dk[:, cols], w[:, half : 2 * half])
        g = g + dot_nt(dv[:, cols], w[:, 2 * half : 3 * half])
    n, r = normalise(tok[...].astype(f32))
    out_ref[...] = (gh[...].astype(f32) + norm_back(n, r, g * vec[6:7, :])).astype(bf16)


def input_grad(joint, fsdp, tok, gh, dq, dk, dv, glow, down, vec):
    tokens, width = tok.shape
    rows = 512
    row = pl.BlockSpec((rows, width), lambda i: (i, 0))
    thin = pl.BlockSpec((rows, LANES), lambda i: (i, 0))
    return weight_call(
        input_kernel,
        "input_grad",
        [(w, (width, 3 * width // 2)) for w in joint],
        [(0, 0, 3 * width // 2), (1, 0, 3 * width // 2)],
        (tokens // rows,),
        [dq, dk, dv, glow, down, vec, tok, gh],
        [row] * 3 + [thin, resident(down), resident(vec), row, row],
        [row],
        [jax.ShapeDtypeStruct((tokens, width), bf16)],
        [],
        6 * tokens * width * width,
        fsdp,
    )[0]


def per_device(
    tokens,
    document_length_list,
    joint_projection_weight,
    attention_out_weight,
    feed_up_weight,
    feed_down_weight,
    frozen_norm_gains,
    biases,
    hidden_up_bias,
    query_down_adapter,
    query_up_adapter,
    value_down_adapter,
    value_up_adapter,
    cotangent,
):
    micro, local, seq, width = tokens.shape
    slots = micro * local
    shards = width // joint_projection_weight.shape[0]
    hidden = feed_down_weight.shape[0]
    tok = tokens.reshape(slots * seq, width)
    cot = cotangent.reshape(slots * seq, width)
    lengths = document_length_list.reshape(slots, -1)

    dp = lax.axis_size("dp")
    chunks = 4
    part = hidden // chunks
    stepped = dp == 4 and shards == 8 and part == LANES and width == shards * LANES

    def gather(x):
        return lax.all_gather(x, "fsdp", axis=0, tiled=True)

    adapters = [query_down_adapter, query_up_adapter, value_down_adapter, value_up_adapter]
    if stepped:
        a, part_a = cut(joint_projection_weight, biases, frozen_norm_gains, hidden_up_bias, dp)
        link = Gather(dp, shards)
        near = link.step_1(part_a)
        shards_here = [joint_projection_weight, feed_up_weight, feed_down_weight, attention_out_weight]
        *shards_here, part_a = after_all(shards_here + [part_a], a)
        b, c, part_b, part_c, down_map, up_map = pack(*shards_here, adapters, chunks, shards, dp)
        b_near = link.step_1(part_b)
        near = after_all(near, part_c)
        a_far = link.all_far(near)
        b_far = link.all_far(b_near)
        c_near = link.step_1(after(part_c, b_near))
        joint = [pieces(a, link.swap(a), [a_far], [link.swap(a_far)])]
        vec = None
    else:
        small = jnp.concatenate([biases, frozen_norm_gains], axis=0)
        small = lax.all_gather(small, "fsdp", axis=1, tiled=True)
        hidden_bias = lax.all_gather(hidden_up_bias, "fsdp", axis=0, tiled=False)
        hidden_bias = [hidden_bias[:, j * part : (j + 1) * part].reshape(1, -1) for j in range(chunks)]
        vec = jnp.concatenate([small] + hidden_bias, axis=0)
        vec = jnp.pad(vec, ((0, 16 - 8 - chunks), (0, 0))).astype(f32)
        third = [width * i // 2 for i in range(6)]
        joint = []
        for i in (0, 1):
            cols = [lax.slice_in_dim(joint_projection_weight, t, t + width // 2, axis=1) for t in third[i::2]]
            joint.append([(gather(jnp.concatenate(cols, axis=1)), 0, 0, "whole")])
        up_parts = feed_up_weight.reshape(-1, shards, chunks, part)
        feeds = []
        for group in ((0,), tuple(range(1, chunks))):
            cols = []
            for j in group:
                cols.append(up_parts[:, :, j, :].reshape(-1, shards * part))
                cols.append(feed_down_weight[j * part : (j + 1) * part])
            if group[0] == 0:
                cols.append(attention_out_weight)
            feeds.append([(gather(jnp.concatenate(cols, axis=1)), 0, 0, "whole")])
        rank = query_down_adapter.shape[1]
        down_map = jnp.concatenate([query_down_adapter, value_down_adapter], axis=1)
        down_map = jnp.pad(down_map, ((0, 0), (0, LANES - 2 * rank)))
        zero = jnp.zeros_like(query_up_adapter)
        up_map = jnp.concatenate(
            [
                jnp.concatenate([query_up_adapter, zero], axis=1),
                jnp.concatenate([zero, value_up_adapter], axis=1),
            ],
            axis=0,
        )
        up_map = jnp.pad(up_map * 8, ((0, LANES - 2 * rank), (0, 0))).astype(bf16)

    q, k, v, low, normed, vec, *kept = heads(joint[0], shards, lengths, tok, down_map, up_map, vec)
    if stepped:
        b_far, *c_near, q = after_all([b_far] + c_near + [q], low)
        b_rest = [link.swap(b), [b_far], [link.swap(b_far)]]
        c_far = link.each_far(c_near)
        joint.append(pieces(b, *b_rest))
    old = [q, k, v] + kept
    q, k, v, att, probs, linv = heads(joint[1], shards, lengths, normed, down_map, up_map, vec, low, old)
    if stepped:
        feeds = [pieces(b, *b_rest, joint_projection_weight.shape[1] // 2, joint_projection_weight.shape[1] // 2)]
        c_other = [link.swap(c_far[0])]
        *c_other, att = after_all(c_other + [att], vec)
    h1, normed_2, o, g = feed_first(feeds, shards, tok, att, cot, vec)
    if stepped:
        *far, o = after_all(c_far[1:] + [o], h1)
        c_other += [link.swap(x) for x in far]
        feeds.append(pieces(c, link.swap(after(c, vec)), c_far[:1] + far, c_other))
    out, gh, ga = feed_last(feeds, shards, h1, normed_2, o, g, cot, vec)

    dq, dk, dv, glow, grads = attend_back(slots, q, k, v, ga, att, probs, linv, low, normed, up_map)
    if stepped:
        total = Gather(dp, shards)
        grads = grads + total.move(grads, lambda d, f: (d, f ^ 1))
        _, a, b, c = total.each_far([grads])
        grads = (grads + a) + (b + c)
        a, b, c = [total.move(grads, lambda d, f, k=k: (d, (f + 2 * k) % shards)) for k in (1, 2, 3)]
        dq = after(dq, grads)
        grad_in = input_grad(joint, shards, tok, gh, dq, dk, dv, glow, down_map, vec)
        a, b, c = after_all([a, b, c], grad_in)
        grads = (grads + b) + (a + c)
    else:
        grads = jnp.sum(lax.all_gather(grads, ("dp", "fsdp"), axis=0, tiled=False), axis=0)
        grad_in = input_grad(joint, shards, tok, gh, dq, dk, dv, glow, down_map, vec)
    return (
        out.reshape(tokens.shape),
        grad_in.reshape(tokens.shape),
        grads[8:12].T,
        grads[0:4],
        grads[12:16].T,
        grads[4:8],
    )


def solution(mesh):
    slots = P(None, ("dp", "fsdp"), None, None)
    return jax.shard_map(
        per_device,
        mesh=mesh,
        in_specs=(
            slots,
            P(None, ("dp", "fsdp"), None),
            P("fsdp", None),
            P("fsdp", None),
            P("fsdp", None),
            P("fsdp", None),
            P(None, "fsdp"),
            P(None, "fsdp"),
            P("fsdp"),
            P(),
            P(),
            P(),
            P(),
            slots,
        ),
        out_specs=(slots, slots, P(), P(), P(), P()),
        check_vma=False,
    )
```

profile of v0, /device:TPU:0, one launch (start us, length us, event | category | flops | bytes accessed | tf_op | source)
XLA Modules:
  0.0 335.3 jit_solution(11580752995610852865)
XLA Ops:
  0.6 2.0 cut.1
  2.7 5.0 %collective-permute-start.3 = (bf16[32,1664]{1,0:T(8,128)(2,1)}, bf16[32,1664]{1,0:T(8,128)(2,1)S(1)}, u32[]{:S(2)}, u32[]{:S(2)}) collective-permute-start(bf16[32,1664]{1,0:T(8,128)(2,1)} %get-tuple-element.65), channel_id=1, source_target_pairs={{0,6},{1,7},{2,0},{3,1},{4,2},{5,3},{6,4},{7,5},{8,14},{9,15},{10,... | collective-permute-start | bytes 319496 | tf_op jit(solution)/shard_map/ppermute | solution.py:88
  7.7 1.0 collective-permute-start.1
  8.7 1.6 copy.26.q_down
  10.3 1.6 copy.27.v_down
  11.9 4.3 %pack.1 = (bf16[128,4608]{1,0:T(8,128)(2,1)}, bf16[128,6144]{1,0:T(8,128)(2,1)}, bf16[32,4608]{1,0:T(8,128)(2,1)}, bf16[32,6144]{1,0:T(8,128)(2,1)}, bf16[1024,1...) custom-call(bf16[128,3072]{1,0:T(8,128)(2,1)} %joint.2, bf16[128,4096]{1,0:T(8,128)(2,1)} %up, bf16[512,1024]{1,0:T(8,128)(2,1)} %down, ...), custom_call_target="tpu_custom_call" | custom-call | tf_op jit(solution)/shard_map/pack/pallas_call | solution.py:237
  16.2 1.1 collective-permute-done.2
  17.4 1.1 pad_maximum_fusion.1
  18.6 3.7 %all-to-all-start = ((bf16[4,96,1664]{2,1,0:T(8,128)(2,1)}), bf16[4,96,1664]{2,1,0:T(8,128)(2,1)S(1)}, u32[]{:S(2)}, u32[]{:S(2)}) async-start(bf16[4,96,1664]{2,1,0:T(8,128)(2,1)} %pad_maximum_fusion.1), calls=%async_computation | async-start | bytes 2555904 | tf_op jit(solution)/shard_map/all_to_all | solution.py:96
  22.3 1.9 collective-permute-start.8
  24.1 1.0 collective-permute-start.7
  25.2 1.5 collective-permute-start.6
  26.7 5.0 %collective-permute-done.8 = bf16[32,4608]{1,0:T(8,128)(2,1)S(1)} collective-permute-done((bf16[32,4608]{1,0:T(8,128)(2,1)S(1)}, bf16[32,4608]{1,0:T(8,128)(2,1)S(1)}, u32[]{:S(2)}, u32[]{:S(2)}) %collective-permute-start.8) | collective-permute-done | bytes 294944 | tf_op jit(solution)/shard_map/ppermute | solution.py:88
  31.7 18.2 %collective-permute-done.7 = bf16[32,4608]{1,0:T(8,128)(2,1)S(1)} collective-permute-done((bf16[32,4608]{1,0:T(8,128)(2,1)S(1)}, bf16[32,4608]{1,0:T(8,128)(2,1)S(1)}, u32[]{:S(2)}, u32[]{:S(2)}) %collective-permute-start.7) | collective-permute-done | bytes 294944 | tf_op jit(solution)/shard_map/ppermute | solution.py:88
  50.2 1.9 pad_maximum_fusion
  52.1 1.1 copy-done.2
  53.2 3.8 %all-to-all-start.1 = ((bf16[4,96,4608]{2,1,0:T(8,128)(2,1)}), bf16[4,96,4608]{2,1,0:T(8,128)(2,1)S(1)}, u32[]{:S(2)}, u32[]{:S(2)}) async-start(bf16[4,96,4608]{2,1,0:T(8,128)(2,1)} %pad_maximum_fusion), calls=%async_computation.1 | async-start | bytes 7077888 | tf_op jit(solution)/shard_map/all_to_all | solution.py:96
  57.5 2.1 collective-permute-start.10
  59.6 2.0 collective-permute-start.9
  61.7 0.7 copy-done.8
  62.4 0.5 copy-done.3
  62.9 26.6 %heads.2 = (bf16[2048,1024]{1,0:T(8,128)(2,1)}, bf16[2048,1024]{1,0:T(8,128)(2,1)}, bf16[2048,1024]{1,0:T(8,128)(2,1)}, bf16[2048,128]{1,0:T(8,128)(2,1)}, bf16[...) custom-call(bf16[128,1664]{1,0:T(8,128)(2,1)} %get-tuple-element.66., ...), custom_call_target="tpu_custom_call" | custom-call | flops 2415919104 | bytes 1048576 | tf_op jit(solution)/shard_map/heads/pallas_call | solution.py:188
  89.5 4.9 %collective-permute-done.10.refs_1_ = bf16[32,6144]{1,0:T(8,128)(2,1)S(1)} collective-permute-done((bf16[32,6144]{1,0:T(8,128)(2,1)}, bf16[32,6144]{1,0:T(8,128)(2,1)S(1)}, u32[]{:S(2)}, u32[]{:S(2)}) %collective-permute-start.10) | collective-permute-done | bytes 393248 | tf_op jit(solution)/shard_map/ppermute | solution.py:88
  94.5 0.7 copy-done.10
  96.1 3.1 stack.1.refs_2_
  99.2 2.5 collective-permute-start.14
  101.7 0.6 collective-permute-start.13
  102.2 1.1 collective-permute-done.15.refs_1_.refs_11_.refs_5_
  103.4 1.7 collective-permute-start.12
  105.1 24.3 %heads.3 = (bf16[2048,1024]{1,0:T(8,128)(2,1)}, bf16[2048,1024]{1,0:T(8,128)(2,1)}, bf16[2048,1024]{1,0:T(8,128)(2,1)}, bf16[2048,1024]{1,0:T(8,128)(2,1)}, bf16...) custom-call(bf16[128,4608]{1,0:T(8,128)(2,1)} %get-tuple-element.87., ...), custom_call_target="tpu_custom_call", output_to_operand_aliasing={{0}: (10, {}), {1}: (11, {}), {2}: (12, {}), {3}: (13, {}),... | custom-call | flops 2415919104 | bytes 1048576 | tf_op jit(solution)/shard_map/heads/pallas_call | solution.py:188
  129.4 33.6 %feed_first.1 = (f32[2048,1024]{1,0:T(8,128)}, bf16[2048,1024]{1,0:T(8,128)(2,1)}, f32[2048,1024]{1,0:T(8,128)}, f32[2048,1024]{1,0:T(8,128)}) custom-call(bf16[128,4608]{1,0:T(8,128)(2,1)} %get-tuple-element.87.refs_0_.refs_10_.refs_4_, bf16[128,4608]{1,0:T(8,128)(2,1)} %copy-done.1, bf16[4,96,4608]{2,1,0:T(8,128)(2,1)} %copy-done, ...), custom_call_target="tpu_custom_call" | custom-call | flops 4831838208 | bytes 1048576 | tf_op jit(solution)/shard_map/feed_first/pallas_call | solution.py:188
  164.0 2.2 collective-permute-done.18.refs_7_
  166.2 1.7 collective-permute-done.19.refs_8_
  167.9 1.7 collective-permute-done.20.refs_9_
  169.6 1.0 copy-done.7
  170.6 86.7 %feed_last.1 = (bf16[2048,1024]{1,0:T(8,128)(2,1)}, bf16[2048,1024]{1,0:T(8,128)(2,1)}, bf16[2048,1024]{1,0:T(8,128)(2,1)}) custom-call(bf16[128,6144]{1,0:T(8,128)(2,1)} %get-tuple-element.79.refs_0_, bf16[128,6144]{1,0:T(8,128)(2,1)} %collective-permute-done.5.refs_1_, bf16[96,6144]{1,0:T(8,128)(2,1)} %stack.1.refs_2_, ...), custom_call_target="tpu_custom_call" | custom-call | flops 4831838208 | bytes 1048576 | tf_op jit(solution)/shard_map/feed_last/pallas_call | solution.py:188
  257.3 35.7 %attend_back.1 = (bf16[2048,1024]{1,0:T(8,128)(2,1)}, bf16[2048,1024]{1,0:T(8,128)(2,1)}, bf16[2048,1024]{1,0:T(8,128)(2,1)}, bf16[2048,128]{1,0:T(8,128)(2,1)}, f32[16,1024]{1,0:T(8,128)}) custom-call(bf16[2048,1024]{1,0:T(8,128)(2,1)} %get-tuple-element.108.q_ref, bf16[2048,1024]{1,0:T(8,128)(2,1)} %get-tuple-element.109.k_ref, ...), custom_call_target="tpu_custom_call" | custom-call | flops 3758096384 | bytes 1048576 | tf_op jit(solution)/shard_map/attend_back/pallas_call | solution.py:593
  293.5 1.1 collective-permute-done.21
  294.6 0.9 add.21
  295.4 2.9 collective-permute-start.24
  298.3 0.6 collective-permute-start.23
  299.0 2.0 collective-permute-done.24
  300.9 1.7 collective-permute-done.23
  302.6 0.6 collective-permute-done.22
  303.2 3.0 collective-permute-start.26
  306.2 1.9 collective-permute-start.25
  308.2 26.2 %input_grad.1 = bf16[2048,1024]{1,0:T(8,128)(2,1)} custom-call(bf16[128,1664]{1,0:T(8,128)(2,1)} %get-tuple-element.66.refs_0_, bf16[128,1664]{1,0:T(8,128)(2,1)} %copy-done.8, bf16[4,96,1664]{2,1,0:T(8,128)(2,1)} %copy-done.2, bf16[4,96,1664]{2,1,0:T(8,128)(2,1)} %copy-done.3, bf16[128,4608]{1,0:T(8,128)(2,1)} %get-tuple-element.87.refs_0_.refs_10_.refs_4_, ...), custom_call_target="tpu_custom_call" | custom-call | flops 1610612736 | bytes 1048576 | tf_op jit(solution)/shard_map/input_grad/pallas_call | solution.py:188
  334.4 0.6 fusion
  (59 shorter events, 3.5 us)
Async XLA Ops:
  2.7 13.6 %collective-permute-start.3 = (bf16[32,1664]{1,0:T(8,128)(2,1)}, bf16[32,1664]{1,0:T(8,128)(2,1)S(1)}, u32[]{:S(2)}, u32[]{:S(2)}) collective-permute-start(bf16[32,1664]{1,0:T(8,128)(2,1)} %get-tuple-element.65), channel_id=1, source_target_pairs={{0,6},{1,7},{2,0},{3,1},{4,2},{5,3},{6,4},{7,5},{8,14},{9,15},{10,... | collective-permute-start | bytes 319496 | tf_op jit(solution)/shard_map/ppermute | solution.py:88
  7.7 9.6 %collective-permute-start.2 = (bf16[32,1664]{1,0:T(8,128)(2,1)}, bf16[32,1664]{1,0:T(8,128)(2,1)S(1)}, u32[]{:S(2)}, u32[]{:S(2)}) collective-permute-start(bf16[32,1664]{1,0:T(8,128)(2,1)} %get-tuple-element.65), channel_id=1, source_target_pairs={{0,4},{1,5},{2,6},{3,7},{4,0},{5,1},{6,2},{7,3},{8,12},{9,13},{10,... | collective-permute-start | bytes 319496 | tf_op jit(solution)/shard_map/ppermute | solution.py:88
  7.7 9.6 %collective-permute-start.1 = (bf16[32,1664]{1,0:T(8,128)(2,1)}, bf16[32,1664]{1,0:T(8,128)(2,1)S(1)}, u32[]{:S(2)}, u32[]{:S(2)}) collective-permute-start(bf16[32,1664]{1,0:T(8,128)(2,1)} %get-tuple-element.65), channel_id=1, source_target_pairs={{0,2},{1,3},{2,4},{3,5},{4,6},{5,7},{6,0},{7,1},{8,10},{9,11},{10,... | collective-permute-start | bytes 319496 | tf_op jit(solution)/shard_map/ppermute | solution.py:88
  16.2 6.0 %copy-start.11 = (bf16[32,4608]{1,0:T(8,128)(2,1)S(1)}, bf16[32,4608]{1,0:T(8,128)(2,1)}, u32[]{:S(2)}) copy-start(bf16[32,4608]{1,0:T(8,128)(2,1)} %get-tuple-element.80) | copy-start | bytes 884740
  18.6 33.5 %all-to-all-start = ((bf16[4,96,1664]{2,1,0:T(8,128)(2,1)}), bf16[4,96,1664]{2,1,0:T(8,128)(2,1)S(1)}, u32[]{:S(2)}, u32[]{:S(2)}) async-start(bf16[4,96,1664]{2,1,0:T(8,128)(2,1)} %pad_maximum_fusion.1), calls=%async_computation | async-start | bytes 2555904 | tf_op jit(solution)/shard_map/all_to_all | solution.py:96
  22.3 9.4 %collective-permute-start.8 = (bf16[32,4608]{1,0:T(8,128)(2,1)S(1)}, bf16[32,4608]{1,0:T(8,128)(2,1)S(1)}, u32[]{:S(2)}, u32[]{:S(2)}) collective-permute-start(bf16[32,4608]{1,0:T(8,128)(2,1)S(1)} %copy-done.11), channel_id=1, source_target_pairs={{0,6},{1,7},{2,0},{3,1},{4,2},{5,3},{6,4},{7,5},{8,14},{9,15},{10,... | collective-permute-start | bytes 884744 | tf_op jit(solution)/shard_map/ppermute | solution.py:88
  24.1 25.8 %collective-permute-start.7 = (bf16[32,4608]{1,0:T(8,128)(2,1)S(1)}, bf16[32,4608]{1,0:T(8,128)(2,1)S(1)}, u32[]{:S(2)}, u32[]{:S(2)}) collective-permute-start(bf16[32,4608]{1,0:T(8,128)(2,1)S(1)} %copy-done.11), channel_id=1, source_target_pairs={{0,4},{1,5},{2,6},{3,7},{4,0},{5,1},{6,2},{7,3},{8,12},{9,13},{10,... | collective-permute-start | bytes 884744 | tf_op jit(solution)/shard_map/ppermute | solution.py:88
  25.2 24.7 %collective-permute-start.6 = (bf16[32,4608]{1,0:T(8,128)(2,1)S(1)}, bf16[32,4608]{1,0:T(8,128)(2,1)S(1)}, u32[]{:S(2)}, u32[]{:S(2)}) collective-permute-start(bf16[32,4608]{1,0:T(8,128)(2,1)S(1)} %copy-done.11), channel_id=1, source_target_pairs={{0,2},{1,3},{2,4},{3,5},{4,6},{5,7},{6,0},{7,1},{8,10},{9,11},{10,... | collective-permute-start | bytes 884744 | tf_op jit(solution)/shard_map/ppermute | solution.py:88
  52.1 1.1 copy-start.2
  53.2 42.4 %all-to-all-start.1 = ((bf16[4,96,4608]{2,1,0:T(8,128)(2,1)}), bf16[4,96,4608]{2,1,0:T(8,128)(2,1)S(1)}, u32[]{:S(2)}, u32[]{:S(2)}) async-start(bf16[4,96,4608]{2,1,0:T(8,128)(2,1)} %pad_maximum_fusion), calls=%async_computation.1 | async-start | bytes 7077888 | tf_op jit(solution)/shard_map/all_to_all | solution.py:96
  57.0 4.7 %collective-permute-start.4 = (bf16[4,96,1664]{2,1,0:T(8,128)(2,1)}, bf16[4,96,1664]{2,1,0:T(8,128)(2,1)S(1)}, u32[]{:S(2)}, u32[]{:S(2)}) collective-permute-start(bf16[4,96,1664]{2,1,0:T(8,128)(2,1)} %copy-done.2), channel_id=1, source_target_pairs={{0,1},{1,0},{2,3},{3,2},{4,5},{5,4},{6,7},{7,6},{8,9},{9,8},{10,11... | collective-permute-start | bytes 3833864 | tf_op jit(solution)/shard_map/ppermute | solution.py:88
  57.0 4.7 %collective-permute-start = (bf16[128,1664]{1,0:T(8,128)(2,1)}, bf16[128,1664]{1,0:T(8,128)(2,1)S(1)}, u32[]{:S(2)}, u32[]{:S(2)}) collective-permute-start(bf16[128,1664]{1,0:T(8,128)(2,1)} %get-tuple-element.66.refs_0_), channel_id=1, source_target_pairs={{0,1},{1,0},{2,3},{3,2},{4,5},{5,4},{6,7},{7,6},{8,9},{9,8},{10,11... | collective-permute-start | bytes 1277960 | tf_op jit(solution)/shard_map/ppermute | solution.py:88
  57.5 32.0 %collective-permute-start.11 = (bf16[32,6144]{1,0:T(8,128)(2,1)}, bf16[32,6144]{1,0:T(8,128)(2,1)S(1)}, u32[]{:S(2)}, u32[]{:S(2)}) collective-permute-start(bf16[32,6144]{1,0:T(8,128)(2,1)} %get-tuple-element.81), channel_id=1, source_target_pairs={{0,6},{1,7},{2,0},{3,1},{4,2},{5,3},{6,4},{7,5},{8,14},{9,15},{10,... | collective-permute-start | bytes 1179656 | tf_op jit(solution)/shard_map/ppermute | solution.py:88
  57.5 37.0 %collective-permute-start.10 = (bf16[32,6144]{1,0:T(8,128)(2,1)}, bf16[32,6144]{1,0:T(8,128)(2,1)S(1)}, u32[]{:S(2)}, u32[]{:S(2)}) collective-permute-start(bf16[32,6144]{1,0:T(8,128)(2,1)} %get-tuple-element.81), channel_id=1, source_target_pairs={{0,4},{1,5},{2,6},{3,7},{4,0},{5,1},{6,2},{7,3},{8,12},{9,13},{10,... | collective-permute-start | bytes 1179656 | tf_op jit(solution)/shard_map/ppermute | solution.py:88
  59.6 35.6 %collective-permute-start.9 = (bf16[32,6144]{1,0:T(8,128)(2,1)}, bf16[32,6144]{1,0:T(8,128)(2,1)}, u32[]{:S(2)}, u32[]{:S(2)}) collective-permute-start(bf16[32,6144]{1,0:T(8,128)(2,1)} %get-tuple-element.81), channel_id=1, source_target_pairs={{0,2},{1,3},{2,4},{3,5},{4,6},{5,7},{6,0},{7,1},{8,10},{9,11},{10,... | collective-permute-start | bytes 1179656 | tf_op jit(solution)/shard_map/ppermute | solution.py:88
  61.6 0.8 copy-start.8
  61.7 1.3 copy-start.3
  89.5 4.9 %copy-start.9 = (bf16[32,6144]{1,0:T(8,128)(2,1)}, bf16[32,6144]{1,0:T(8,128)(2,1)S(1)}, u32[]{:S(2)}) copy-start(bf16[32,6144]{1,0:T(8,128)(2,1)S(1)} %collective-permute-done.11.refs_2_) | copy-start | bytes 1179652
  94.5 0.7 copy-start.10
  95.6 9.5 %copy-start = (bf16[4,96,4608]{2,1,0:T(8,128)(2,1)}, bf16[4,96,4608]{2,1,0:T(8,128)(2,1)S(1)}, u32[]{:S(2)}) copy-start(bf16[4,96,4608]{2,1,0:T(8,128)(2,1)S(1)} %all-to-all-done.1.refs_2_.refs_12_.refs_6_) | copy-start | bytes 10616836
  95.6 9.4 %collective-permute-start.16 = (bf16[4,96,4608]{2,1,0:T(8,128)(2,1)S(1)}, bf16[4,96,4608]{2,1,0:T(8,128)(2,1)}, u32[]{:S(2)}, u32[]{:S(2)}) collective-permute-start(bf16[4,96,4608]{2,1,0:T(8,128)(2,1)S(1)} %all-to-all-done.1.refs_2_.refs_12_.refs_6_), channel_id=1, source_target_pairs={{0,1},{1,0},{2,3},{3,2},{4,5},{5,4},{6,7},{7,6},{8,9},{9,8},{10,11... | collective-permute-start | bytes 10616840 | tf_op jit(solution)/shard_map/ppermute | solution.py:88
  95.6 7.7 %collective-permute-start.15 = (bf16[128,4608]{1,0:T(8,128)(2,1)}, bf16[128,4608]{1,0:T(8,128)(2,1)S(1)}, u32[]{:S(2)}, u32[]{:S(2)}) collective-permute-start(bf16[128,4608]{1,0:T(8,128)(2,1)} %get-tuple-element.87.refs_0_.refs_10_.refs_4_), channel_id=1, source_target_pairs={{0,1},{1,0},{2,3},{3,2},{4,5},{5,4},{6,7},{7,6},{8,9},{9,8},{10,11... | collective-permute-start | bytes 3538952 | tf_op jit(solution)/shard_map/ppermute | solution.py:88
  99.2 30.1 %collective-permute-start.17 = (bf16[96,6144]{1,0:T(8,128)(2,1)}, bf16[96,6144]{1,0:T(8,128)(2,1)S(1)}, u32[]{:S(2)}, u32[]{:S(2)}) collective-permute-start(bf16[96,6144]{1,0:T(8,128)(2,1)} %stack.1.refs_2_), channel_id=1, source_target_pairs={{0,1},{1,0},{2,3},{3,2},{4,5},{5,4},{6,7},{7,6},{8,9},{9,8},{10,11... | collective-permute-start | bytes 3538952 | tf_op jit(solution)/shard_map/ppermute | solution.py:88
  99.2 63.8 %collective-permute-start.14 = (bf16[96,6144]{1,0:T(8,128)(2,1)}, bf16[96,6144]{1,0:T(8,128)(2,1)}, u32[]{:S(2)}, u32[]{:S(2)}) collective-permute-start(bf16[96,6144]{1,0:T(8,128)(2,1)} %stack.1.refs_2_), channel_id=1, source_target_pairs={{0,24},{1,25},{2,26},{3,27},{4,28},{5,29},{6,30},{7,31},{8,16},{9,... | collective-permute-start | bytes 3538952 | tf_op jit(solution)/shard_map/ppermute | solution.py:88
  101.7 61.3 %collective-permute-start.13 = (bf16[96,6144]{1,0:T(8,128)(2,1)}, bf16[96,6144]{1,0:T(8,128)(2,1)}, u32[]{:S(2)}, u32[]{:S(2)}) collective-permute-start(bf16[96,6144]{1,0:T(8,128)(2,1)} %stack.1.refs_2_), channel_id=1, source_target_pairs={{0,16},{1,17},{2,18},{3,19},{4,20},{5,21},{6,22},{7,23},{8,24},{9,... | collective-permute-start | bytes 3538952 | tf_op jit(solution)/shard_map/ppermute | solution.py:88
  103.4 1.7 copy-start.1
  103.4 59.6 %collective-permute-start.12 = (bf16[96,6144]{1,0:T(8,128)(2,1)}, bf16[96,6144]{1,0:T(8,128)(2,1)}, u32[]{:S(2)}, u32[]{:S(2)}) collective-permute-start(bf16[96,6144]{1,0:T(8,128)(2,1)} %stack.1.refs_2_), channel_id=1, source_target_pairs={{0,8},{1,9},{2,10},{3,11},{4,12},{5,13},{6,14},{7,15},{8,0},{9,1},... | collective-permute-start | bytes 3538952 | tf_op jit(solution)/shard_map/ppermute | solution.py:88
  105.0 59.0 %collective-permute-start.5 = (bf16[128,6144]{1,0:T(8,128)(2,1)}, bf16[128,6144]{1,0:T(8,128)(2,1)}, u32[]{:S(2)}, u32[]{:S(2)}) collective-permute-start(bf16[128,6144]{1,0:T(8,128)(2,1)} %get-tuple-element.79.refs_0_), channel_id=1, source_target_pairs={{0,1},{1,0},{2,3},{3,2},{4,5},{5,4},{6,7},{7,6},{8,9},{9,8},{10,11... | collective-permute-start | bytes 4718600 | tf_op jit(solution)/shard_map/ppermute | solution.py:88
  129.4 33.6 %copy-start.4 = (bf16[96,6144]{1,0:T(8,128)(2,1)}, bf16[96,6144]{1,0:T(8,128)(2,1)S(1)}, u32[]{:S(2)}) copy-start(bf16[96,6144]{1,0:T(8,128)(2,1)S(1)} %collective-permute-done.17.refs_6_) | copy-start | bytes 3538948
  163.0 3.2 collective-permute-start.18
  163.5 4.4 %collective-permute-start.19 = (bf16[96,6144]{1,0:T(8,128)(2,1)}, bf16[96,6144]{1,0:T(8,128)(2,1)S(1)}, u32[]{:S(2)}, u32[]{:S(2)}) collective-permute-start(bf16[96,6144]{1,0:T(8,128)(2,1)} %collective-permute-done.13.refs_4_), channel_id=1, source_target_pairs={{0,1},{1,0},{2,3},{3,2},{4,5},{5,4},{6,7},{7,6},{8,9},{9,8},{10,11... | collective-permute-start | bytes 3538952 | tf_op jit(solution)/shard_map/ppermute | solution.py:88
  163.6 6.0 %collective-permute-start.20 = (bf16[96,6144]{1,0:T(8,128)(2,1)}, bf16[96,6144]{1,0:T(8,128)(2,1)S(1)}, u32[]{:S(2)}, u32[]{:S(2)}) collective-permute-start(bf16[96,6144]{1,0:T(8,128)(2,1)} %collective-permute-done.14.refs_5_), channel_id=1, source_target_pairs={{0,1},{1,0},{2,3},{3,2},{4,5},{5,4},{6,7},{7,6},{8,9},{9,8},{10,11... | collective-permute-start | bytes 3538952 | tf_op jit(solution)/shard_map/ppermute | solution.py:88
  166.2 3.4 %copy-start.5 = (bf16[96,6144]{1,0:T(8,128)(2,1)}, bf16[96,6144]{1,0:T(8,128)(2,1)S(1)}, u32[]{:S(2)}) copy-start(bf16[96,6144]{1,0:T(8,128)(2,1)S(1)} %collective-permute-done.18.refs_7_) | copy-start | bytes 3538948
  167.9 1.7 copy-start.6
  169.6 1.0 copy-start.7
  293.0 1.6 collective-permute-start.21
  295.4 5.5 %collective-permute-start.24 = (f32[16,1024]{1,0:T(8,128)S(1)}, f32[16,1024]{1,0:T(8,128)S(1)}, u32[]{:S(2)}, u32[]{:S(2)}) collective-permute-start(f32[16,1024]{1,0:T(8,128)S(1)} %add.21), channel_id=1, source_target_pairs={{0,24},{1,25},{2,26},{3,27},{4,28},{5,29},{6,30},{7,31},{8,16},{9,... | collective-permute-start | bytes 196616 | tf_op jit(solution)/shard_map/ppermute | solution.py:88
  298.3 4.3 %collective-permute-start.23 = (f32[16,1024]{1,0:T(8,128)S(1)}, f32[16,1024]{1,0:T(8,128)S(1)}, u32[]{:S(2)}, u32[]{:S(2)}) collective-permute-start(f32[16,1024]{1,0:T(8,128)S(1)} %add.21), channel_id=1, source_target_pairs={{0,16},{1,17},{2,18},{3,19},{4,20},{5,21},{6,22},{7,23},{8,24},{9,... | collective-permute-start | bytes 196616 | tf_op jit(solution)/shard_map/ppermute | solution.py:88
  298.9 4.3 %collective-permute-start.22 = (f32[16,1024]{1,0:T(8,128)S(1)}, f32[16,1024]{1,0:T(8,128)S(1)}, u32[]{:S(2)}, u32[]{:S(2)}) collective-permute-start(f32[16,1024]{1,0:T(8,128)S(1)} %add.21), channel_id=1, source_target_pairs={{0,8},{1,9},{2,10},{3,11},{4,12},{5,13},{6,14},{7,15},{8,0},{9,1},... | collective-permute-start | bytes 196616 | tf_op jit(solution)/shard_map/ppermute | solution.py:88
  303.2 31.2 %collective-permute-start.27 = (f32[16,1024]{1,0:T(8,128)S(1)}, f32[16,1024]{1,0:T(8,128)S(1)}, u32[]{:S(2)}, u32[]{:S(2)}) collective-permute-start(f32[16,1024]{1,0:T(8,128)S(1)} %add_add_fusion.1), channel_id=1, source_target_pairs={{0,6},{1,7},{2,0},{3,1},{4,2},{5,3},{6,4},{7,5},{8,14},{9,15},{10,... | collective-permute-start | bytes 196616 | tf_op jit(solution)/shard_map/ppermute | solution.py:88
  303.2 31.1 %collective-permute-start.26 = (f32[16,1024]{1,0:T(8,128)S(1)}, f32[16,1024]{1,0:T(8,128)S(1)}, u32[]{:S(2)}, u32[]{:S(2)}) collective-permute-start(f32[16,1024]{1,0:T(8,128)S(1)} %add_add_fusion.1), channel_id=1, source_target_pairs={{0,4},{1,5},{2,6},{3,7},{4,0},{5,1},{6,2},{7,3},{8,12},{9,13},{10,... | collective-permute-start | bytes 196616 | tf_op jit(solution)/shard_map/ppermute | solution.py:88
  306.2 28.2 %collective-permute-start.25 = (f32[16,1024]{1,0:T(8,128)S(1)}, f32[16,1024]{1,0:T(8,128)S(1)}, u32[]{:S(2)}, u32[]{:S(2)}) collective-permute-start(f32[16,1024]{1,0:T(8,128)S(1)} %add_add_fusion.1), channel_id=1, source_target_pairs={{0,2},{1,3},{2,4},{3,5},{4,6},{5,7},{6,0},{7,1},{8,10},{9,11},{10,... | collective-permute-start | bytes 196616 | tf_op jit(solution)/shard_map/ppermute | solution.py:88
where the time goes:
time: 338 us; the launch traced here: 335 us
  Pallas kernels  242 us (72%)
  waiting for transfers between devices  41.6 us (12%)
  starting transfers between devices  37.9 us (11%)
  local copies, waits for them, and re-layouts  8.22 us (2%)
  other arithmetic  3.96 us (1%)
    pallas_call x5, Pallas kernels, weight_call(): pl.pallas_call(body, grid=grid, in_specs=[pl.BlockSpec(memory_space=pltpu...  197 us
    ppermute x28, waiting for transfers between devices, move(): lax.ppermute(x, ('dp', 'fsdp'), ring_pairs(self.dp, self.fsdp, where))  41.2 us
    pallas_call x1, Pallas kernels, attend_back(): pl.pallas_call(functools.partial(attend_back_kernel, pairs, blocks), grid...  35.7 us
    ppermute x28, starting transfers between devices, move(): lax.ppermute(x, ('dp', 'fsdp'), ring_pairs(self.dp, self.fsdp, where))  30.4 us
    pallas_call x3, Pallas kernels, local_call(): pl.pallas_call(kernel, out_shape=[jax.ShapeDtypeStruct(s, bf16) for s in...  9.5 us
    all_to_all x2, starting transfers between devices, all_far(): lax.all_to_all(jnp.concatenate(near, axis=1), 'dp', 0, 0, tiled=False)  7.53 us
    unnamed x26, local copies, waits for them, and re-layouts  7.26 us
  transfers between devices with their start and end apart: 30, of which 13 were waited for; matrix products, arithmetic and copies ran while one was open for 2% of the time, Pallas kernels for 35%

commit v1 on v0

--- a/solution.py
+++ b/solution.py
@@ -792,6 +792,8 @@
         b_far = link.all_far(b_near)
         c_near = link.step_1(after(part_c, b_near))
         joint = [pieces(a, link.swap(a), [a_far], [link.swap(a_far)])]
+        b_other = link.swap(after(b, a_far))
+        tok = after(tok, b_other)
         vec = None
     else:
         small = jnp.concatenate([biases, frozen_norm_gains], axis=0)
@@ -831,7 +833,7 @@
     q, k, v, low, normed, vec, *kept = heads(joint[0], shards, lengths, tok, down_map, up_map, vec)
     if stepped:
         b_far, *c_near, q = after_all([b_far] + c_near + [q], low)
-        b_rest = [link.swap(b), [b_far], [link.swap(b_far)]]
+        b_rest = [b_other, [b_far], [link.swap(b_far)]]
         c_far = link.each_far(c_near)
         joint.append(pieces(b, *b_rest))
     old = [q, k, v] + kept

time: 338 us -> 336 us (level)
    unnamed x26 -> x24, local copies, waits for them, and re-layouts: 7.26 us -> 7.28 us
where the time goes in v1:
time: 336 us; the launch traced here: 333 us
  Pallas kernels  242 us (72%)
  waiting for transfers between devices  42 us (12%)
  starting transfers between devices  35.4 us (11%)
  local copies, waits for them, and re-layouts  8.24 us (2%)
  other arithmetic  3.96 us (1%)
    pallas_call x5, Pallas kernels, weight_call(): pl.pallas_call(body, grid=grid, in_specs=[pl.BlockSpec(memory_space=pltpu...  197 us
    ppermute x28, waiting for transfers between devices, move(): lax.ppermute(x, ('dp', 'fsdp'), ring_pairs(self.dp, self.fsdp, where))  42 us
    pallas_call x1, Pallas kernels, attend_back(): pl.pallas_call(functools.partial(attend_back_kernel, pairs, blocks), grid...  35.7 us
    ppermute x28, starting transfers between devices, move(): lax.ppermute(x, ('dp', 'fsdp'), ring_pairs(self.dp, self.fsdp, where))  27.8 us
    pallas_call x3, Pallas kernels, local_call(): pl.pallas_call(kernel, out_shape=[jax.ShapeDtypeStruct(s, bf16) for s in...  9.65 us
    all_to_all x2, starting transfers between devices, all_far(): lax.all_to_all(jnp.concatenate(near, axis=1), 'dp', 0, 0, tiled=False)  7.53 us
    unnamed x24, local copies, waits for them, and re-layouts  7.28 us
  transfers between devices with their start and end apart: 30, of which 13 were waited for; matrix products, arithmetic and copies ran while one was open for 2% of the time, Pallas kernels for 35%

profile of v1, /device:TPU:0, one launch (start us, length us, event | category | flops | bytes accessed | tf_op | source)
XLA Modules:
  0.0 332.9 jit_solution(5836623443168968588)
XLA Ops:
  0.6 2.1 cut.1
  2.7 5.0 %collective-permute-start.3 = (bf16[32,1664]{1,0:T(8,128)(2,1)}, bf16[32,1664]{1,0:T(8,128)(2,1)S(1)}, u32[]{:S(2)}, u32[]{:S(2)}) collective-permute-start(bf16[32,1664]{1,0:T(8,128)(2,1)} %get-tuple-element.67), channel_id=1, source_target_pairs={{0,6},{1,7},{2,0},{3,1},{4,2},{5,3},{6,4},{7,5},{8,14},{9,15},{10,... | collective-permute-start | bytes 319496 | tf_op jit(solution)/shard_map/ppermute | solution.py:88
  7.7 1.0 collective-permute-start.1
  8.8 1.6 copy.26.q_down
  10.3 1.6 copy.27.v_down
  11.9 4.3 %pack.1 = (bf16[128,4608]{1,0:T(8,128)(2,1)}, bf16[128,6144]{1,0:T(8,128)(2,1)}, bf16[32,4608]{1,0:T(8,128)(2,1)}, bf16[32,6144]{1,0:T(8,128)(2,1)}, bf16[1024,1...) custom-call(bf16[128,3072]{1,0:T(8,128)(2,1)} %joint.2, bf16[128,4096]{1,0:T(8,128)(2,1)} %up, bf16[512,1024]{1,0:T(8,128)(2,1)} %down, ...), custom_call_target="tpu_custom_call" | custom-call | tf_op jit(solution)/shard_map/pack/pallas_call | solution.py:237
  16.2 1.1 collective-permute-done.2
  17.4 1.1 pad_maximum_fusion.1
  18.6 3.7 %all-to-all-start = ((bf16[4,96,1664]{2,1,0:T(8,128)(2,1)}), bf16[4,96,1664]{2,1,0:T(8,128)(2,1)S(1)}, u32[]{:S(2)}, u32[]{:S(2)}) async-start(bf16[4,96,1664]{2,1,0:T(8,128)(2,1)} %pad_maximum_fusion.1), calls=%async_computation | async-start | bytes 2555904 | tf_op jit(solution)/shard_map/all_to_all | solution.py:96
  22.3 1.9 collective-permute-start.9
  24.1 1.0 collective-permute-start.8
  25.2 1.5 collective-permute-start.7
  26.7 5.0 %collective-permute-done.9 = bf16[32,4608]{1,0:T(8,128)(2,1)S(1)} collective-permute-done((bf16[32,4608]{1,0:T(8,128)(2,1)S(1)}, bf16[32,4608]{1,0:T(8,128)(2,1)S(1)}, u32[]{:S(2)}, u32[]{:S(2)}) %collective-permute-start.9) | collective-permute-done | bytes 294944 | tf_op jit(solution)/shard_map/ppermute | solution.py:88
  31.7 18.2 %collective-permute-done.8 = bf16[32,4608]{1,0:T(8,128)(2,1)S(1)} collective-permute-done((bf16[32,4608]{1,0:T(8,128)(2,1)S(1)}, bf16[32,4608]{1,0:T(8,128)(2,1)S(1)}, u32[]{:S(2)}, u32[]{:S(2)}) %collective-permute-start.8) | collective-permute-done | bytes 294944 | tf_op jit(solution)/shard_map/ppermute | solution.py:88
  50.2 1.9 pad_maximum_fusion
  52.1 1.1 copy-done.1
  53.2 3.8 %all-to-all-start.1 = ((bf16[4,96,4608]{2,1,0:T(8,128)(2,1)}), bf16[4,96,4608]{2,1,0:T(8,128)(2,1)S(1)}, u32[]{:S(2)}, u32[]{:S(2)}) async-start(bf16[4,96,4608]{2,1,0:T(8,128)(2,1)} %pad_maximum_fusion), calls=%async_computation.1 | async-start | bytes 7077888 | tf_op jit(solution)/shard_map/all_to_all | solution.py:96
  57.6 2.1 collective-permute-start.11
  59.7 1.5 collective-permute-done.5.refs_1_.refs_11_.refs_5_
  61.2 0.5 collective-permute-start.10
  61.7 0.8 collective-permute-done.refs_1_
  62.5 0.7 copy-done.7
  63.2 0.5 copy-done.3
  63.8 26.6 %heads.2 = (bf16[2048,1024]{1,0:T(8,128)(2,1)}, bf16[2048,1024]{1,0:T(8,128)(2,1)}, bf16[2048,1024]{1,0:T(8,128)(2,1)}, bf16[2048,128]{1,0:T(8,128)(2,1)}, bf16[...) custom-call(bf16[128,1664]{1,0:T(8,128)(2,1)} %get-tuple-element.68., ...), custom_call_target="tpu_custom_call" | custom-call | flops 2415919104 | bytes 1048576 | tf_op jit(solution)/shard_map/heads/pallas_call | solution.py:188
  90.4 4.5 %collective-permute-done.11.refs_1_ = bf16[32,6144]{1,0:T(8,128)(2,1)S(1)} collective-permute-done((bf16[32,6144]{1,0:T(8,128)(2,1)}, bf16[32,6144]{1,0:T(8,128)(2,1)S(1)}, u32[]{:S(2)}, u32[]{:S(2)}) %collective-permute-start.11) | collective-permute-done | bytes 393248 | tf_op jit(solution)/shard_map/ppermute | solution.py:88
  94.9 0.7 copy-done.9
  95.8 3.3 stack.1.refs_2_
  99.1 3.0 collective-permute-start.15
  102.1 0.6 collective-permute-start.14
  102.7 24.3 %heads.3 = (bf16[2048,1024]{1,0:T(8,128)(2,1)}, bf16[2048,1024]{1,0:T(8,128)(2,1)}, bf16[2048,1024]{1,0:T(8,128)(2,1)}, bf16[2048,1024]{1,0:T(8,128)(2,1)}, bf16...) custom-call(bf16[128,4608]{1,0:T(8,128)(2,1)} %get-tuple-element.79., ...), custom_call_target="tpu_custom_call", output_to_operand_aliasing={{0}: (10, {}), {1}: (11, {}), {2}: (12, {}), {3}: (13, {}),... | custom-call | flops 2415919104 | bytes 1048576 | tf_op jit(solution)/shard_map/heads/pallas_call | solution.py:188
  127.0 33.1 %feed_first.1 = (f32[2048,1024]{1,0:T(8,128)}, bf16[2048,1024]{1,0:T(8,128)(2,1)}, f32[2048,1024]{1,0:T(8,128)}, f32[2048,1024]{1,0:T(8,128)}) custom-call(bf16[128,4608]{1,0:T(8,128)(2,1)} %get-tuple-element.79.refs_0_.refs_10_.refs_4_, bf16[128,4608]{1,0:T(8,128)(2,1)} %collective-permute-done.5.refs_1_.refs_11_.refs_5_, bf16[4,96,4608]{2,1,0:T(8,128)(2,1)} %copy-done, ...), custom_call_target="tpu_custom_call" | custom-call | flops 4831838208 | bytes 1048576 | tf_op jit(solution)/shard_map/feed_first/pallas_call | solution.py:188
  161.2 2.2 collective-permute-done.18.refs_7_
  163.4 1.7 collective-permute-done.19.refs_8_
  165.1 1.7 collective-permute-done.20.refs_9_
  166.8 1.0 copy-done.6
  167.8 86.7 %feed_last.1 = (bf16[2048,1024]{1,0:T(8,128)(2,1)}, bf16[2048,1024]{1,0:T(8,128)(2,1)}, bf16[2048,1024]{1,0:T(8,128)(2,1)}) custom-call(bf16[128,6144]{1,0:T(8,128)(2,1)} %get-tuple-element.84.refs_0_, bf16[128,6144]{1,0:T(8,128)(2,1)} %copy-done.2, bf16[96,6144]{1,0:T(8,128)(2,1)} %stack.1.refs_2_, bf16[96,6144]{1,0:T(8,128)(2,1)} %collective-permute-done.13.refs_3_, ...), custom_call_target="tpu_custom_call" | custom-call | flops 4831838208 | bytes 1048576 | tf_op jit(solution)/shard_map/feed_last/pallas_call | solution.py:188
  254.5 35.7 %attend_back.1 = (bf16[2048,1024]{1,0:T(8,128)(2,1)}, bf16[2048,1024]{1,0:T(8,128)(2,1)}, bf16[2048,1024]{1,0:T(8,128)(2,1)}, bf16[2048,128]{1,0:T(8,128)(2,1)}, f32[16,1024]{1,0:T(8,128)}) custom-call(bf16[2048,1024]{1,0:T(8,128)(2,1)} %get-tuple-element.112.q_ref, bf16[2048,1024]{1,0:T(8,128)(2,1)} %get-tuple-element.113.k_ref, ...), custom_call_target="tpu_custom_call" | custom-call | flops 3758096384 | bytes 1048576 | tf_op jit(solution)/shard_map/attend_back/pallas_call | solution.py:593
  290.6 1.1 collective-permute-done.21
  291.8 0.9 add.21
  292.6 3.0 collective-permute-start.24
  295.6 0.6 collective-permute-start.23
  296.2 2.0 collective-permute-done.24
  298.2 1.7 collective-permute-done.23
  299.9 0.6 collective-permute-done.22
  300.5 3.3 collective-permute-start.26
  303.8 1.9 collective-permute-start.25
  305.8 26.2 %input_grad.1 = bf16[2048,1024]{1,0:T(8,128)(2,1)} custom-call(bf16[128,1664]{1,0:T(8,128)(2,1)} %get-tuple-element.68.refs_0_, bf16[128,1664]{1,0:T(8,128)(2,1)} %copy-done.7, bf16[4,96,1664]{2,1,0:T(8,128)(2,1)} %copy-done.1, bf16[4,96,1664]{2,1,0:T(8,128)(2,1)} %copy-done.3, bf16[128,4608]{1,0:T(8,128)(2,1)} %get-tuple-element.79.refs_0_.refs_10_.refs_4_, ...), custom_call_target="tpu_custom_call" | custom-call | flops 1610612736 | bytes 1048576 | tf_op jit(solution)/shard_map/input_grad/pallas_call | solution.py:188
  332.0 0.6 fusion
  (57 shorter events, 2.8 us)
Async XLA Ops:
  2.7 13.6 %collective-permute-start.3 = (bf16[32,1664]{1,0:T(8,128)(2,1)}, bf16[32,1664]{1,0:T(8,128)(2,1)S(1)}, u32[]{:S(2)}, u32[]{:S(2)}) collective-permute-start(bf16[32,1664]{1,0:T(8,128)(2,1)} %get-tuple-element.67), channel_id=1, source_target_pairs={{0,6},{1,7},{2,0},{3,1},{4,2},{5,3},{6,4},{7,5},{8,14},{9,15},{10,... | collective-permute-start | bytes 319496 | tf_op jit(solution)/shard_map/ppermute | solution.py:88
  7.7 9.6 %collective-permute-start.2 = (bf16[32,1664]{1,0:T(8,128)(2,1)}, bf16[32,1664]{1,0:T(8,128)(2,1)S(1)}, u32[]{:S(2)}, u32[]{:S(2)}) collective-permute-start(bf16[32,1664]{1,0:T(8,128)(2,1)} %get-tuple-element.67), channel_id=1, source_target_pairs={{0,4},{1,5},{2,6},{3,7},{4,0},{5,1},{6,2},{7,3},{8,12},{9,13},{10,... | collective-permute-start | bytes 319496 | tf_op jit(solution)/shard_map/ppermute | solution.py:88
  7.7 9.6 %collective-permute-start.1 = (bf16[32,1664]{1,0:T(8,128)(2,1)}, bf16[32,1664]{1,0:T(8,128)(2,1)S(1)}, u32[]{:S(2)}, u32[]{:S(2)}) collective-permute-start(bf16[32,1664]{1,0:T(8,128)(2,1)} %get-tuple-element.67), channel_id=1, source_target_pairs={{0,2},{1,3},{2,4},{3,5},{4,6},{5,7},{6,0},{7,1},{8,10},{9,11},{10,... | collective-permute-start | bytes 319496 | tf_op jit(solution)/shard_map/ppermute | solution.py:88
  16.2 6.0 %copy-start.10 = (bf16[32,4608]{1,0:T(8,128)(2,1)S(1)}, bf16[32,4608]{1,0:T(8,128)(2,1)}, u32[]{:S(2)}) copy-start(bf16[32,4608]{1,0:T(8,128)(2,1)} %get-tuple-element.85) | copy-start | bytes 884740
  18.6 33.5 %all-to-all-start = ((bf16[4,96,1664]{2,1,0:T(8,128)(2,1)}), bf16[4,96,1664]{2,1,0:T(8,128)(2,1)S(1)}, u32[]{:S(2)}, u32[]{:S(2)}) async-start(bf16[4,96,1664]{2,1,0:T(8,128)(2,1)} %pad_maximum_fusion.1), calls=%async_computation | async-start | bytes 2555904 | tf_op jit(solution)/shard_map/all_to_all | solution.py:96
  22.3 9.4 %collective-permute-start.9 = (bf16[32,4608]{1,0:T(8,128)(2,1)S(1)}, bf16[32,4608]{1,0:T(8,128)(2,1)S(1)}, u32[]{:S(2)}, u32[]{:S(2)}) collective-permute-start(bf16[32,4608]{1,0:T(8,128)(2,1)S(1)} %copy-done.10), channel_id=1, source_target_pairs={{0,6},{1,7},{2,0},{3,1},{4,2},{5,3},{6,4},{7,5},{8,14},{9,15},{10,... | collective-permute-start | bytes 884744 | tf_op jit(solution)/shard_map/ppermute | solution.py:88
  24.1 25.8 %collective-permute-start.8 = (bf16[32,4608]{1,0:T(8,128)(2,1)S(1)}, bf16[32,4608]{1,0:T(8,128)(2,1)S(1)}, u32[]{:S(2)}, u32[]{:S(2)}) collective-permute-start(bf16[32,4608]{1,0:T(8,128)(2,1)S(1)} %copy-done.10), channel_id=1, source_target_pairs={{0,4},{1,5},{2,6},{3,7},{4,0},{5,1},{6,2},{7,3},{8,12},{9,13},{10,... | collective-permute-start | bytes 884744 | tf_op jit(solution)/shard_map/ppermute | solution.py:88
  25.2 24.7 %collective-permute-start.7 = (bf16[32,4608]{1,0:T(8,128)(2,1)S(1)}, bf16[32,4608]{1,0:T(8,128)(2,1)S(1)}, u32[]{:S(2)}, u32[]{:S(2)}) collective-permute-start(bf16[32,4608]{1,0:T(8,128)(2,1)S(1)} %copy-done.10), channel_id=1, source_target_pairs={{0,2},{1,3},{2,4},{3,5},{4,6},{5,7},{6,0},{7,1},{8,10},{9,11},{10,... | collective-permute-start | bytes 884744 | tf_op jit(solution)/shard_map/ppermute | solution.py:88
  52.1 1.1 copy-start.1
  53.2 42.5 %all-to-all-start.1 = ((bf16[4,96,4608]{2,1,0:T(8,128)(2,1)}), bf16[4,96,4608]{2,1,0:T(8,128)(2,1)S(1)}, u32[]{:S(2)}, u32[]{:S(2)}) async-start(bf16[4,96,4608]{2,1,0:T(8,128)(2,1)} %pad_maximum_fusion), calls=%async_computation.1 | async-start | bytes 7077888 | tf_op jit(solution)/shard_map/all_to_all | solution.py:96
  57.0 4.2 %collective-permute-start.5 = (bf16[128,4608]{1,0:T(8,128)(2,1)}, bf16[128,4608]{1,0:T(8,128)(2,1)}, u32[]{:S(2)}, u32[]{:S(2)}) collective-permute-start(bf16[128,4608]{1,0:T(8,128)(2,1)} %get-tuple-element.79.refs_0_.refs_10_.refs_4_), channel_id=1, source_target_pairs={{0,1},{1,0},{2,3},{3,2},{4,5},{5,4},{6,7},{7,6},{8,9},{9,8},{10,11... | collective-permute-start | bytes 3538952 | tf_op jit(solution)/shard_map/ppermute | solution.py:88
  57.0 5.5 %collective-permute-start.4 = (bf16[4,96,1664]{2,1,0:T(8,128)(2,1)}, bf16[4,96,1664]{2,1,0:T(8,128)(2,1)S(1)}, u32[]{:S(2)}, u32[]{:S(2)}) collective-permute-start(bf16[4,96,1664]{2,1,0:T(8,128)(2,1)} %copy-done.1), channel_id=1, source_target_pairs={{0,1},{1,0},{2,3},{3,2},{4,5},{5,4},{6,7},{7,6},{8,9},{9,8},{10,11... | collective-permute-start | bytes 3833864 | tf_op jit(solution)/shard_map/ppermute | solution.py:88
  57.5 5.0 %collective-permute-start = (bf16[128,1664]{1,0:T(8,128)(2,1)}, bf16[128,1664]{1,0:T(8,128)(2,1)S(1)}, u32[]{:S(2)}, u32[]{:S(2)}) collective-permute-start(bf16[128,1664]{1,0:T(8,128)(2,1)} %get-tuple-element.68.refs_0_), channel_id=1, source_target_pairs={{0,1},{1,0},{2,3},{3,2},{4,5},{5,4},{6,7},{7,6},{8,9},{9,8},{10,11... | collective-permute-start | bytes 1277960 | tf_op jit(solution)/shard_map/ppermute | solution.py:88
  57.6 32.8 %collective-permute-start.12 = (bf16[32,6144]{1,0:T(8,128)(2,1)}, bf16[32,6144]{1,0:T(8,128)(2,1)S(1)}, u32[]{:S(2)}, u32[]{:S(2)}) collective-permute-start(bf16[32,6144]{1,0:T(8,128)(2,1)} %get-tuple-element.86), channel_id=1, source_target_pairs={{0,6},{1,7},{2,0},{3,1},{4,2},{5,3},{6,4},{7,5},{8,14},{9,15},{10,... | collective-permute-start | bytes 1179656 | tf_op jit(solution)/shard_map/ppermute | solution.py:88
  57.6 37.3 %collective-permute-start.11 = (bf16[32,6144]{1,0:T(8,128)(2,1)}, bf16[32,6144]{1,0:T(8,128)(2,1)S(1)}, u32[]{:S(2)}, u32[]{:S(2)}) collective-permute-start(bf16[32,6144]{1,0:T(8,128)(2,1)} %get-tuple-element.86), channel_id=1, source_target_pairs={{0,4},{1,5},{2,6},{3,7},{4,0},{5,1},{6,2},{7,3},{8,12},{9,13},{10,... | collective-permute-start | bytes 1179656 | tf_op jit(solution)/shard_map/ppermute | solution.py:88
  61.2 34.5 %collective-permute-start.10 = (bf16[32,6144]{1,0:T(8,128)(2,1)}, bf16[32,6144]{1,0:T(8,128)(2,1)}, u32[]{:S(2)}, u32[]{:S(2)}) collective-permute-start(bf16[32,6144]{1,0:T(8,128)(2,1)} %get-tuple-element.86), channel_id=1, source_target_pairs={{0,2},{1,3},{2,4},{3,5},{4,6},{5,7},{6,0},{7,1},{8,10},{9,11},{10,... | collective-permute-start | bytes 1179656 | tf_op jit(solution)/shard_map/ppermute | solution.py:88
  62.5 0.8 copy-start.7
  62.5 1.3 copy-start.3
  90.4 4.6 %copy-start.8 = (bf16[32,6144]{1,0:T(8,128)(2,1)}, bf16[32,6144]{1,0:T(8,128)(2,1)S(1)}, u32[]{:S(2)}) copy-start(bf16[32,6144]{1,0:T(8,128)(2,1)S(1)} %collective-permute-done.12.refs_2_) | copy-start | bytes 1179652
  94.9 0.7 copy-start.9
  95.7 7.0 %copy-start = (bf16[4,96,4608]{2,1,0:T(8,128)(2,1)}, bf16[4,96,4608]{2,1,0:T(8,128)(2,1)S(1)}, u32[]{:S(2)}) copy-start(bf16[4,96,4608]{2,1,0:T(8,128)(2,1)S(1)} %all-to-all-done.1.refs_2_.refs_12_.refs_6_) | copy-start | bytes 10616836
  95.7 7.0 %collective-permute-start.16 = (bf16[4,96,4608]{2,1,0:T(8,128)(2,1)S(1)}, bf16[4,96,4608]{2,1,0:T(8,128)(2,1)}, u32[]{:S(2)}, u32[]{:S(2)}) collective-permute-start(bf16[4,96,4608]{2,1,0:T(8,128)(2,1)S(1)} %all-to-all-done.1.refs_2_.refs_12_.refs_6_), channel_id=1, source_target_pairs={{0,1},{1,0},{2,3},{3,2},{4,5},{5,4},{6,7},{7,6},{8,9},{9,8},{10,11... | collective-permute-start | bytes 10616840 | tf_op jit(solution)/shard_map/ppermute | solution.py:88
  99.0 28.0 %collective-permute-start.17 = (bf16[96,6144]{1,0:T(8,128)(2,1)}, bf16[96,6144]{1,0:T(8,128)(2,1)}, u32[]{:S(2)}, u32[]{:S(2)}) collective-permute-start(bf16[96,6144]{1,0:T(8,128)(2,1)} %stack.1.refs_2_), channel_id=1, source_target_pairs={{0,1},{1,0},{2,3},{3,2},{4,5},{5,4},{6,7},{7,6},{8,9},{9,8},{10,11... | collective-permute-start | bytes 3538952 | tf_op jit(solution)/shard_map/ppermute | solution.py:88
  99.1 61.0 %collective-permute-start.15 = (bf16[96,6144]{1,0:T(8,128)(2,1)}, bf16[96,6144]{1,0:T(8,128)(2,1)}, u32[]{:S(2)}, u32[]{:S(2)}) collective-permute-start(bf16[96,6144]{1,0:T(8,128)(2,1)} %stack.1.refs_2_), channel_id=1, source_target_pairs={{0,24},{1,25},{2,26},{3,27},{4,28},{5,29},{6,30},{7,31},{8,16},{9,... | collective-permute-start | bytes 3538952 | tf_op jit(solution)/shard_map/ppermute | solution.py:88
  102.1 58.0 %collective-permute-start.14 = (bf16[96,6144]{1,0:T(8,128)(2,1)}, bf16[96,6144]{1,0:T(8,128)(2,1)}, u32[]{:S(2)}, u32[]{:S(2)}) collective-permute-start(bf16[96,6144]{1,0:T(8,128)(2,1)} %stack.1.refs_2_), channel_id=1, source_target_pairs={{0,16},{1,17},{2,18},{3,19},{4,20},{5,21},{6,22},{7,23},{8,24},{9,... | collective-permute-start | bytes 3538952 | tf_op jit(solution)/shard_map/ppermute | solution.py:88
  102.7 57.5 %collective-permute-start.13 = (bf16[96,6144]{1,0:T(8,128)(2,1)}, bf16[96,6144]{1,0:T(8,128)(2,1)}, u32[]{:S(2)}, u32[]{:S(2)}) collective-permute-start(bf16[96,6144]{1,0:T(8,128)(2,1)} %stack.1.refs_2_), channel_id=1, source_target_pairs={{0,8},{1,9},{2,10},{3,11},{4,12},{5,13},{6,14},{7,15},{8,0},{9,1},... | collective-permute-start | bytes 3538952 | tf_op jit(solution)/shard_map/ppermute | solution.py:88
  102.7 58.5 %collective-permute-start.6 = (bf16[128,6144]{1,0:T(8,128)(2,1)}, bf16[128,6144]{1,0:T(8,128)(2,1)S(1)}, u32[]{:S(2)}, u32[]{:S(2)}) collective-permute-start(bf16[128,6144]{1,0:T(8,128)(2,1)} %get-tuple-element.84.refs_0_), channel_id=1, source_target_pairs={{0,1},{1,0},{2,3},{3,2},{4,5},{5,4},{6,7},{7,6},{8,9},{9,8},{10,11... | collective-permute-start | bytes 4718600 | tf_op jit(solution)/shard_map/ppermute | solution.py:88
  160.2 3.2 collective-permute-start.18
  160.7 4.4 %collective-permute-start.19 = (bf16[96,6144]{1,0:T(8,128)(2,1)}, bf16[96,6144]{1,0:T(8,128)(2,1)S(1)}, u32[]{:S(2)}, u32[]{:S(2)}) collective-permute-start(bf16[96,6144]{1,0:T(8,128)(2,1)} %collective-permute-done.14.refs_4_), channel_id=1, source_target_pairs={{0,1},{1,0},{2,3},{3,2},{4,5},{5,4},{6,7},{7,6},{8,9},{9,8},{10,11... | collective-permute-start | bytes 3538952 | tf_op jit(solution)/shard_map/ppermute | solution.py:88
  160.8 6.0 %collective-permute-start.20 = (bf16[96,6144]{1,0:T(8,128)(2,1)}, bf16[96,6144]{1,0:T(8,128)(2,1)S(1)}, u32[]{:S(2)}, u32[]{:S(2)}) collective-permute-start(bf16[96,6144]{1,0:T(8,128)(2,1)} %collective-permute-done.15.refs_5_), channel_id=1, source_target_pairs={{0,1},{1,0},{2,3},{3,2},{4,5},{5,4},{6,7},{7,6},{8,9},{9,8},{10,11... | collective-permute-start | bytes 3538952 | tf_op jit(solution)/shard_map/ppermute | solution.py:88
  161.2 5.5 %copy-start.2 = (bf16[128,6144]{1,0:T(8,128)(2,1)}, bf16[128,6144]{1,0:T(8,128)(2,1)S(1)}, u32[]{:S(2)}) copy-start(bf16[128,6144]{1,0:T(8,128)(2,1)S(1)} %collective-permute-done.6.refs_1_) | copy-start | bytes 4718596
  163.4 3.4 %copy-start.4 = (bf16[96,6144]{1,0:T(8,128)(2,1)}, bf16[96,6144]{1,0:T(8,128)(2,1)S(1)}, u32[]{:S(2)}) copy-start(bf16[96,6144]{1,0:T(8,128)(2,1)S(1)} %collective-permute-done.18.refs_7_) | copy-start | bytes 3538948
  165.1 1.7 copy-start.5
  166.8 1.0 copy-start.6
  290.2 1.6 collective-permute-start.21
  292.6 5.6 %collective-permute-start.24 = (f32[16,1024]{1,0:T(8,128)S(1)}, f32[16,1024]{1,0:T(8,128)S(1)}, u32[]{:S(2)}, u32[]{:S(2)}) collective-permute-start(f32[16,1024]{1,0:T(8,128)S(1)} %add.21), channel_id=1, source_target_pairs={{0,24},{1,25},{2,26},{3,27},{4,28},{5,29},{6,30},{7,31},{8,16},{9,... | collective-permute-start | bytes 196616 | tf_op jit(solution)/shard_map/ppermute | solution.py:88
  295.6 4.3 %collective-permute-start.23 = (f32[16,1024]{1,0:T(8,128)S(1)}, f32[16,1024]{1,0:T(8,128)S(1)}, u32[]{:S(2)}, u32[]{:S(2)}) collective-permute-start(f32[16,1024]{1,0:T(8,128)S(1)} %add.21), channel_id=1, source_target_pairs={{0,16},{1,17},{2,18},{3,19},{4,20},{5,21},{6,22},{7,23},{8,24},{9,... | collective-permute-start | bytes 196616 | tf_op jit(solution)/shard_map/ppermute | solution.py:88
  296.2 4.3 %collective-permute-start.22 = (f32[16,1024]{1,0:T(8,128)S(1)}, f32[16,1024]{1,0:T(8,128)S(1)}, u32[]{:S(2)}, u32[]{:S(2)}) collective-permute-start(f32[16,1024]{1,0:T(8,128)S(1)} %add.21), channel_id=1, source_target_pairs={{0,8},{1,9},{2,10},{3,11},{4,12},{5,13},{6,14},{7,15},{8,0},{9,1},... | collective-permute-start | bytes 196616 | tf_op jit(solution)/shard_map/ppermute | solution.py:88
  300.4 31.5 %collective-permute-start.27 = (f32[16,1024]{1,0:T(8,128)S(1)}, f32[16,1024]{1,0:T(8,128)S(1)}, u32[]{:S(2)}, u32[]{:S(2)}) collective-permute-start(f32[16,1024]{1,0:T(8,128)S(1)} %add_add_fusion.1), channel_id=1, source_target_pairs={{0,6},{1,7},{2,0},{3,1},{4,2},{5,3},{6,4},{7,5},{8,14},{9,15},{10,... | collective-permute-start | bytes 196616 | tf_op jit(solution)/shard_map/ppermute | solution.py:88
  300.5 31.4 %collective-permute-start.26 = (f32[16,1024]{1,0:T(8,128)S(1)}, f32[16,1024]{1,0:T(8,128)S(1)}, u32[]{:S(2)}, u32[]{:S(2)}) collective-permute-start(f32[16,1024]{1,0:T(8,128)S(1)} %add_add_fusion.1), channel_id=1, source_target_pairs={{0,4},{1,5},{2,6},{3,7},{4,0},{5,1},{6,2},{7,3},{8,12},{9,13},{10,... | collective-permute-start | bytes 196616 | tf_op jit(solution)/shard_map/ppermute | solution.py:88
  303.8 28.2 %collective-permute-start.25 = (f32[16,1024]{1,0:T(8,128)S(1)}, f32[16,1024]{1,0:T(8,128)S(1)}, u32[]{:S(2)}, u32[]{:S(2)}) collective-permute-start(f32[16,1024]{1,0:T(8,128)S(1)} %add_add_fusion.1), channel_id=1, source_target_pairs={{0,2},{1,3},{2,4},{3,5},{4,6},{5,7},{6,0},{7,1},{8,10},{9,11},{10,... | collective-permute-start | bytes 196616 | tf_op jit(solution)/shard_map/ppermute | solution.py:88

commit v2 on v1

--- a/solution.py
+++ b/solution.py
@@ -832,7 +832,8 @@
 
     q, k, v, low, normed, vec, *kept = heads(joint[0], shards, lengths, tok, down_map, up_map, vec)
     if stepped:
-        b_far, *c_near, q = after_all([b_far] + c_near + [q], low)
+        b_far, q = after_all([b_far, q], low)
+        c_near = after_all(c_near, q)
         b_rest = [b_other, [b_far], [link.swap(b_far)]]
         c_far = link.each_far(c_near)
         joint.append(pieces(b, *b_rest))

time: 336 us -> 371 us (1.10)
  waiting for transfers between devices: 42 us -> 78.1 us
    ppermute x28, waiting for transfers between devices: 42 us -> 72.9 us  [move(): lax.ppermute(x, ('dp', 'fsdp'), ring_pairs(self.dp, self.fsdp, where))]
    all_to_all x2, waiting for transfers between devices: 0.01 us -> 5.2 us  [all_far(): lax.all_to_all(jnp.concatenate(near, axis=1), 'dp', 0, 0, tiled=False)]
    unnamed x24 -> x26, local copies, waits for them, and re-layouts: 7.28 us -> 7.98 us
  transfers between devices with their start and end apart: 30 -> 30, of which waited for: 13 -> 14; matrix products, arithmetic and copies ran while one was open for 2% -> 1% of each run, Pallas kernels for 35% -> 32%
where the time goes in v2:
time: 371 us; the launch traced here: 369 us
  Pallas kernels  241 us (65%)
  waiting for transfers between devices  78.1 us (21%)
  starting transfers between devices  35.3 us (10%)
  local copies, waits for them, and re-layouts  8.94 us (2%)
  other arithmetic  3.96 us (1%)
    pallas_call x5, Pallas kernels, weight_call(): pl.pallas_call(body, grid=grid, in_specs=[pl.BlockSpec(memory_space=pltpu...  197 us
    ppermute x28, waiting for transfers between devices, move(): lax.ppermute(x, ('dp', 'fsdp'), ring_pairs(self.dp, self.fsdp, where))  72.9 us
    pallas_call x1, Pallas kernels, attend_back(): pl.pallas_call(functools.partial(attend_back_kernel, pairs, blocks), grid...  35.7 us
    ppermute x28, starting transfers between devices, move(): lax.ppermute(x, ('dp', 'fsdp'), ring_pairs(self.dp, self.fsdp, where))  27.8 us
    pallas_call x3, Pallas kernels, local_call(): pl.pallas_call(kernel, out_shape=[jax.ShapeDtypeStruct(s, bf16) for s in...  8.76 us
    unnamed x26, local copies, waits for them, and re-layouts  7.98 us
    all_to_all x2, starting transfers between devices, all_far(): lax.all_to_all(jnp.concatenate(near, axis=1), 'dp', 0, 0, tiled=False)  7.53 us
  transfers between devices with their start and end apart: 30, of which 14 were waited for; matrix products, arithmetic and copies ran while one was open for 1% of the time, Pallas kernels for 32%

profile of v2, /device:TPU:0, one launch (start us, length us, event | category | flops | bytes accessed | tf_op | source)
XLA Modules:
  0.0 368.8 jit_solution(2895278851901059107)
XLA Ops:
  0.6 2.0 cut.1
  2.7 5.0 %collective-permute-start.3 = (bf16[32,1664]{1,0:T(8,128)(2,1)}, bf16[32,1664]{1,0:T(8,128)(2,1)S(1)}, u32[]{:S(2)}, u32[]{:S(2)}) collective-permute-start(bf16[32,1664]{1,0:T(8,128)(2,1)} %get-tuple-element.67), channel_id=1, source_target_pairs={{0,6},{1,7},{2,0},{3,1},{4,2},{5,3},{6,4},{7,5},{8,14},{9,15},{10,... | collective-permute-start | bytes 319496 | tf_op jit(solution)/shard_map/ppermute | solution.py:88
  7.7 1.0 collective-permute-start.1
  8.7 1.6 copy.26.q_down
  10.3 1.6 copy.27.v_down
  11.9 4.3 %pack.1 = (bf16[128,4608]{1,0:T(8,128)(2,1)}, bf16[128,6144]{1,0:T(8,128)(2,1)}, bf16[32,4608]{1,0:T(8,128)(2,1)}, bf16[32,6144]{1,0:T(8,128)(2,1)}, bf16[1024,1...) custom-call(bf16[128,3072]{1,0:T(8,128)(2,1)} %joint.2, bf16[128,4096]{1,0:T(8,128)(2,1)} %up, bf16[512,1024]{1,0:T(8,128)(2,1)} %down, ...), custom_call_target="tpu_custom_call" | custom-call | tf_op jit(solution)/shard_map/pack/pallas_call | solution.py:237
  16.2 1.1 collective-permute-done.2
  17.4 1.1 pad_maximum_fusion.1
  18.6 3.7 %all-to-all-start = ((bf16[4,96,1664]{2,1,0:T(8,128)(2,1)}), bf16[4,96,1664]{2,1,0:T(8,128)(2,1)S(1)}, u32[]{:S(2)}, u32[]{:S(2)}) async-start(bf16[4,96,1664]{2,1,0:T(8,128)(2,1)} %pad_maximum_fusion.1), calls=%async_computation | async-start | bytes 2555904 | tf_op jit(solution)/shard_map/all_to_all | solution.py:96
  22.3 1.9 collective-permute-start.9
  24.1 1.0 collective-permute-start.8
  25.2 1.5 collective-permute-start.7
  26.7 5.0 %collective-permute-done.9 = bf16[32,4608]{1,0:T(8,128)(2,1)S(1)} collective-permute-done((bf16[32,4608]{1,0:T(8,128)(2,1)S(1)}, bf16[32,4608]{1,0:T(8,128)(2,1)S(1)}, u32[]{:S(2)}, u32[]{:S(2)}) %collective-permute-start.9) | collective-permute-done | bytes 294944 | tf_op jit(solution)/shard_map/ppermute | solution.py:88
  31.7 18.2 %collective-permute-done.8 = bf16[32,4608]{1,0:T(8,128)(2,1)S(1)} collective-permute-done((bf16[32,4608]{1,0:T(8,128)(2,1)S(1)}, bf16[32,4608]{1,0:T(8,128)(2,1)S(1)}, u32[]{:S(2)}, u32[]{:S(2)}) %collective-permute-start.8) | collective-permute-done | bytes 294944 | tf_op jit(solution)/shard_map/ppermute | solution.py:88
  50.2 1.9 pad_maximum_fusion
  52.1 1.1 copy-done.1
  53.2 3.8 %all-to-all-start.1 = ((bf16[4,96,4608]{2,1,0:T(8,128)(2,1)}), bf16[4,96,4608]{2,1,0:T(8,128)(2,1)S(1)}, u32[]{:S(2)}, u32[]{:S(2)}) async-start(bf16[4,96,4608]{2,1,0:T(8,128)(2,1)} %pad_maximum_fusion), calls=%async_computation.1 | async-start | bytes 7077888 | tf_op jit(solution)/shard_map/all_to_all | solution.py:96
  57.6 5.0 %collective-permute-done.5.refs_1_.refs_11_.refs_5_ = bf16[128,4608]{1,0:T(8,128)(2,1)} collective-permute-done((bf16[128,4608]{1,0:T(8,128)(2,1)}, bf16[128,4608]{1,0:T(8,128)(2,1)}, u32[]{:S(2)}, u32[]{:S(2)}) %collective-permute-start.5) | collective-permute-done | bytes 1179680 | tf_op jit(solution)/shard_map/ppermute | solution.py:88
  62.6 0.7 copy-done.7
  63.8 26.6 %heads.2 = (bf16[2048,1024]{1,0:T(8,128)(2,1)}, bf16[2048,1024]{1,0:T(8,128)(2,1)}, bf16[2048,1024]{1,0:T(8,128)(2,1)}, bf16[2048,128]{1,0:T(8,128)(2,1)}, bf16[...) custom-call(bf16[128,1664]{1,0:T(8,128)(2,1)} %get-tuple-element.68., ...), custom_call_target="tpu_custom_call" | custom-call | flops 2415919104 | bytes 1048576 | tf_op jit(solution)/shard_map/heads/pallas_call | solution.py:188
  90.4 5.2 %all-to-all-done.1.refs_2_.refs_12_.refs_6_ = bf16[4,96,4608]{2,1,0:T(8,128)(2,1)S(1)} async-done(((bf16[4,96,4608]{2,1,0:T(8,128)(2,1)}), bf16[4,96,4608]{2,1,0:T(8,128)(2,1)S(1)}, u32[]{:S(2)}, u32[]{:S(2)}) %all-to-all-start.1) | async-done | bytes 3538976 | tf_op jit(solution)/shard_map/all_to_all | solution.py:96
  95.6 4.2 %collective-permute-start.11 = (bf16[32,6144]{1,0:T(8,128)(2,1)}, bf16[32,6144]{1,0:T(8,128)(2,1)S(1)}, u32[]{:S(2)}, u32[]{:S(2)}) collective-permute-start(bf16[32,6144]{1,0:T(8,128)(2,1)} %get-tuple-element.86), channel_id=1, source_target_pairs={{0,4},{1,5},{2,6},{3,7},{4,0},{5,1},{6,2},{7,3},{8,12},{9,13},{10,... | collective-permute-start | bytes 1179656 | tf_op jit(solution)/shard_map/ppermute | solution.py:88
  99.9 2.0 collective-permute-start.10
  101.8 6.0 %collective-permute-done.12.refs_2_ = bf16[32,6144]{1,0:T(8,128)(2,1)S(1)} collective-permute-done((bf16[32,6144]{1,0:T(8,128)(2,1)}, bf16[32,6144]{1,0:T(8,128)(2,1)S(1)}, u32[]{:S(2)}, u32[]{:S(2)}) %collective-permute-start.12) | collective-permute-done | bytes 393248 | tf_op jit(solution)/shard_map/ppermute | solution.py:88
  107.9 27.2 %collective-permute-done.11.refs_1_ = bf16[32,6144]{1,0:T(8,128)(2,1)S(1)} collective-permute-done((bf16[32,6144]{1,0:T(8,128)(2,1)}, bf16[32,6144]{1,0:T(8,128)(2,1)S(1)}, u32[]{:S(2)}, u32[]{:S(2)}) %collective-permute-start.11) | collective-permute-done | bytes 393248 | tf_op jit(solution)/shard_map/ppermute | solution.py:88
  135.1 0.7 copy-done.9
  135.8 0.7 copy-done.10
  136.5 2.4 stack.1.refs_2_
  138.9 1.4 collective-permute-start.15
  140.3 1.5 collective-permute-start.14
  141.8 0.6 collective-permute-start.13
  142.4 24.3 %heads.3 = (bf16[2048,1024]{1,0:T(8,128)(2,1)}, bf16[2048,1024]{1,0:T(8,128)(2,1)}, bf16[2048,1024]{1,0:T(8,128)(2,1)}, bf16[2048,1024]{1,0:T(8,128)(2,1)}, bf16...) custom-call(bf16[128,4608]{1,0:T(8,128)(2,1)} %get-tuple-element.79., ...), custom_call_target="tpu_custom_call", output_to_operand_aliasing={{0}: (10, {}), {1}: (11, {}), {2}: (12, {}), {3}: (13, {}),... | custom-call | flops 2415919104 | bytes 1048576 | tf_op jit(solution)/shard_map/heads/pallas_call | solution.py:188
  166.7 33.2 %feed_first.1 = (f32[2048,1024]{1,0:T(8,128)}, bf16[2048,1024]{1,0:T(8,128)(2,1)}, f32[2048,1024]{1,0:T(8,128)}, f32[2048,1024]{1,0:T(8,128)}) custom-call(bf16[128,4608]{1,0:T(8,128)(2,1)} %get-tuple-element.79.refs_0_.refs_10_.refs_4_, bf16[128,4608]{1,0:T(8,128)(2,1)} %collective-permute-done.5.refs_1_.refs_11_.refs_5_, bf16[4,96,4608]{2,1,0:T(8,128)(2,1)} %copy-done, ...), custom_call_target="tpu_custom_call" | custom-call | flops 4831838208 | bytes 1048576 | tf_op jit(solution)/shard_map/feed_first/pallas_call | solution.py:188
  201.0 2.2 collective-permute-done.18.refs_7_
  203.1 1.7 collective-permute-done.19.refs_8_
  204.8 1.7 collective-permute-done.20.refs_9_
  206.5 1.0 copy-done.6
  207.5 86.7 %feed_last.1 = (bf16[2048,1024]{1,0:T(8,128)(2,1)}, bf16[2048,1024]{1,0:T(8,128)(2,1)}, bf16[2048,1024]{1,0:T(8,128)(2,1)}) custom-call(bf16[128,6144]{1,0:T(8,128)(2,1)} %get-tuple-element.84.refs_0_, bf16[128,6144]{1,0:T(8,128)(2,1)} %copy-done.2, bf16[96,6144]{1,0:T(8,128)(2,1)} %stack.1.refs_2_, bf16[96,6144]{1,0:T(8,128)(2,1)} %collective-permute-done.13.refs_3_, ...), custom_call_target="tpu_custom_call" | custom-call | flops 4831838208 | bytes 1048576 | tf_op jit(solution)/shard_map/feed_last/pallas_call | solution.py:188
  294.2 35.7 %attend_back.1 = (bf16[2048,1024]{1,0:T(8,128)(2,1)}, bf16[2048,1024]{1,0:T(8,128)(2,1)}, bf16[2048,1024]{1,0:T(8,128)(2,1)}, bf16[2048,128]{1,0:T(8,128)(2,1)}, f32[16,1024]{1,0:T(8,128)}) custom-call(bf16[2048,1024]{1,0:T(8,128)(2,1)} %get-tuple-element.112.q_ref, bf16[2048,1024]{1,0:T(8,128)(2,1)} %get-tuple-element.113.k_ref, ...), custom_call_target="tpu_custom_call" | custom-call | flops 3758096384 | bytes 1048576 | tf_op jit(solution)/shard_map/attend_back/pallas_call | solution.py:593
  330.4 1.1 collective-permute-done.21
  331.5 0.9 add.21
  332.4 1.5 collective-permute-start.24
  333.8 1.5 collective-permute-start.23
  335.9 1.9 collective-permute-done.24
  337.8 1.3 collective-permute-done.23
  339.7 1.9 collective-permute-start.25
  341.7 26.2 %input_grad.1 = bf16[2048,1024]{1,0:T(8,128)(2,1)} custom-call(bf16[128,1664]{1,0:T(8,128)(2,1)} %get-tuple-element.68.refs_0_, bf16[128,1664]{1,0:T(8,128)(2,1)} %copy-done.7, bf16[4,96,1664]{2,1,0:T(8,128)(2,1)} %copy-done.1, bf16[4,96,1664]{2,1,0:T(8,128)(2,1)} %copy-done.3, bf16[128,4608]{1,0:T(8,128)(2,1)} %get-tuple-element.79.refs_0_.refs_10_.refs_4_, ...), custom_call_target="tpu_custom_call" | custom-call | flops 1610612736 | bytes 1048576 | tf_op jit(solution)/shard_map/input_grad/pallas_call | solution.py:188
  367.9 0.6 fusion
  (59 shorter events, 4.2 us)
Async XLA Ops:
  2.7 13.6 %collective-permute-start.3 = (bf16[32,1664]{1,0:T(8,128)(2,1)}, bf16[32,1664]{1,0:T(8,128)(2,1)S(1)}, u32[]{:S(2)}, u32[]{:S(2)}) collective-permute-start(bf16[32,1664]{1,0:T(8,128)(2,1)} %get-tuple-element.67), channel_id=1, source_target_pairs={{0,6},{1,7},{2,0},{3,1},{4,2},{5,3},{6,4},{7,5},{8,14},{9,15},{10,... | collective-permute-start | bytes 319496 | tf_op jit(solution)/shard_map/ppermute | solution.py:88
  7.7 9.6 %collective-permute-start.2 = (bf16[32,1664]{1,0:T(8,128)(2,1)}, bf16[32,1664]{1,0:T(8,128)(2,1)S(1)}, u32[]{:S(2)}, u32[]{:S(2)}) collective-permute-start(bf16[32,1664]{1,0:T(8,128)(2,1)} %get-tuple-element.67), channel_id=1, source_target_pairs={{0,4},{1,5},{2,6},{3,7},{4,0},{5,1},{6,2},{7,3},{8,12},{9,13},{10,... | collective-permute-start | bytes 319496 | tf_op jit(solution)/shard_map/ppermute | solution.py:88
  7.7 9.6 %collective-permute-start.1 = (bf16[32,1664]{1,0:T(8,128)(2,1)}, bf16[32,1664]{1,0:T(8,128)(2,1)S(1)}, u32[]{:S(2)}, u32[]{:S(2)}) collective-permute-start(bf16[32,1664]{1,0:T(8,128)(2,1)} %get-tuple-element.67), channel_id=1, source_target_pairs={{0,2},{1,3},{2,4},{3,5},{4,6},{5,7},{6,0},{7,1},{8,10},{9,11},{10,... | collective-permute-start | bytes 319496 | tf_op jit(solution)/shard_map/ppermute | solution.py:88
  16.2 6.0 %copy-start.11 = (bf16[32,4608]{1,0:T(8,128)(2,1)S(1)}, bf16[32,4608]{1,0:T(8,128)(2,1)}, u32[]{:S(2)}) copy-start(bf16[32,4608]{1,0:T(8,128)(2,1)} %get-tuple-element.85) | copy-start | bytes 884740
  18.6 33.5 %all-to-all-start = ((bf16[4,96,1664]{2,1,0:T(8,128)(2,1)}), bf16[4,96,1664]{2,1,0:T(8,128)(2,1)S(1)}, u32[]{:S(2)}, u32[]{:S(2)}) async-start(bf16[4,96,1664]{2,1,0:T(8,128)(2,1)} %pad_maximum_fusion.1), calls=%async_computation | async-start | bytes 2555904 | tf_op jit(solution)/shard_map/all_to_all | solution.py:96
  22.3 9.4 %collective-permute-start.9 = (bf16[32,4608]{1,0:T(8,128)(2,1)S(1)}, bf16[32,4608]{1,0:T(8,128)(2,1)S(1)}, u32[]{:S(2)}, u32[]{:S(2)}) collective-permute-start(bf16[32,4608]{1,0:T(8,128)(2,1)S(1)} %copy-done.11), channel_id=1, source_target_pairs={{0,6},{1,7},{2,0},{3,1},{4,2},{5,3},{6,4},{7,5},{8,14},{9,15},{10,... | collective-permute-start | bytes 884744 | tf_op jit(solution)/shard_map/ppermute | solution.py:88
  24.1 25.8 %collective-permute-start.8 = (bf16[32,4608]{1,0:T(8,128)(2,1)S(1)}, bf16[32,4608]{1,0:T(8,128)(2,1)S(1)}, u32[]{:S(2)}, u32[]{:S(2)}) collective-permute-start(bf16[32,4608]{1,0:T(8,128)(2,1)S(1)} %copy-done.11), channel_id=1, source_target_pairs={{0,4},{1,5},{2,6},{3,7},{4,0},{5,1},{6,2},{7,3},{8,12},{9,13},{10,... | collective-permute-start | bytes 884744 | tf_op jit(solution)/shard_map/ppermute | solution.py:88
  25.2 24.7 %collective-permute-start.7 = (bf16[32,4608]{1,0:T(8,128)(2,1)S(1)}, bf16[32,4608]{1,0:T(8,128)(2,1)S(1)}, u32[]{:S(2)}, u32[]{:S(2)}) collective-permute-start(bf16[32,4608]{1,0:T(8,128)(2,1)S(1)} %copy-done.11), channel_id=1, source_target_pairs={{0,2},{1,3},{2,4},{3,5},{4,6},{5,7},{6,0},{7,1},{8,10},{9,11},{10,... | collective-permute-start | bytes 884744 | tf_op jit(solution)/shard_map/ppermute | solution.py:88
  52.1 1.1 copy-start.1
  53.2 42.4 %all-to-all-start.1 = ((bf16[4,96,4608]{2,1,0:T(8,128)(2,1)}), bf16[4,96,4608]{2,1,0:T(8,128)(2,1)S(1)}, u32[]{:S(2)}, u32[]{:S(2)}) async-start(bf16[4,96,4608]{2,1,0:T(8,128)(2,1)} %pad_maximum_fusion), calls=%async_computation.1 | async-start | bytes 7077888 | tf_op jit(solution)/shard_map/all_to_all | solution.py:96
  57.0 5.6 %collective-permute-start.4 = (bf16[4,96,1664]{2,1,0:T(8,128)(2,1)}, bf16[4,96,1664]{2,1,0:T(8,128)(2,1)S(1)}, u32[]{:S(2)}, u32[]{:S(2)}) collective-permute-start(bf16[4,96,1664]{2,1,0:T(8,128)(2,1)} %copy-done.1), channel_id=1, source_target_pairs={{0,1},{1,0},{2,3},{3,2},{4,5},{5,4},{6,7},{7,6},{8,9},{9,8},{10,11... | collective-permute-start | bytes 3833864 | tf_op jit(solution)/shard_map/ppermute | solution.py:88
  57.0 5.5 %collective-permute-start.5 = (bf16[128,4608]{1,0:T(8,128)(2,1)}, bf16[128,4608]{1,0:T(8,128)(2,1)}, u32[]{:S(2)}, u32[]{:S(2)}) collective-permute-start(bf16[128,4608]{1,0:T(8,128)(2,1)} %get-tuple-element.79.refs_0_.refs_10_.refs_4_), channel_id=1, source_target_pairs={{0,1},{1,0},{2,3},{3,2},{4,5},{5,4},{6,7},{7,6},{8,9},{9,8},{10,11... | collective-permute-start | bytes 3538952 | tf_op jit(solution)/shard_map/ppermute | solution.py:88
  57.5 5.0 %collective-permute-start = (bf16[128,1664]{1,0:T(8,128)(2,1)}, bf16[128,1664]{1,0:T(8,128)(2,1)S(1)}, u32[]{:S(2)}, u32[]{:S(2)}) collective-permute-start(bf16[128,1664]{1,0:T(8,128)(2,1)} %get-tuple-element.68.refs_0_), channel_id=1, source_target_pairs={{0,1},{1,0},{2,3},{3,2},{4,5},{5,4},{6,7},{7,6},{8,9},{9,8},{10,11... | collective-permute-start | bytes 1277960 | tf_op jit(solution)/shard_map/ppermute | solution.py:88
  62.5 0.8 copy-start.7
  62.6 1.3 copy-start.3
  95.6 46.8 %copy-start = (bf16[4,96,4608]{2,1,0:T(8,128)(2,1)}, bf16[4,96,4608]{2,1,0:T(8,128)(2,1)S(1)}, u32[]{:S(2)}) copy-start(bf16[4,96,4608]{2,1,0:T(8,128)(2,1)S(1)} %all-to-all-done.1.refs_2_.refs_12_.refs_6_) | copy-start | bytes 10616836
  95.6 46.8 %collective-permute-start.16 = (bf16[4,96,4608]{2,1,0:T(8,128)(2,1)S(1)}, bf16[4,96,4608]{2,1,0:T(8,128)(2,1)}, u32[]{:S(2)}, u32[]{:S(2)}) collective-permute-start(bf16[4,96,4608]{2,1,0:T(8,128)(2,1)S(1)} %all-to-all-done.1.refs_2_.refs_12_.refs_6_), channel_id=1, source_target_pairs={{0,1},{1,0},{2,3},{3,2},{4,5},{5,4},{6,7},{7,6},{8,9},{9,8},{10,11... | collective-permute-start | bytes 10616840 | tf_op jit(solution)/shard_map/ppermute | solution.py:88
  95.6 12.3 %collective-permute-start.12 = (bf16[32,6144]{1,0:T(8,128)(2,1)}, bf16[32,6144]{1,0:T(8,128)(2,1)S(1)}, u32[]{:S(2)}, u32[]{:S(2)}) collective-permute-start(bf16[32,6144]{1,0:T(8,128)(2,1)} %get-tuple-element.86), channel_id=1, source_target_pairs={{0,6},{1,7},{2,0},{3,1},{4,2},{5,3},{6,4},{7,5},{8,14},{9,15},{10,... | collective-permute-start | bytes 1179656 | tf_op jit(solution)/shard_map/ppermute | solution.py:88
  95.6 39.4 %collective-permute-start.11 = (bf16[32,6144]{1,0:T(8,128)(2,1)}, bf16[32,6144]{1,0:T(8,128)(2,1)S(1)}, u32[]{:S(2)}, u32[]{:S(2)}) collective-permute-start(bf16[32,6144]{1,0:T(8,128)(2,1)} %get-tuple-element.86), channel_id=1, source_target_pairs={{0,4},{1,5},{2,6},{3,7},{4,0},{5,1},{6,2},{7,3},{8,12},{9,13},{10,... | collective-permute-start | bytes 1179656 | tf_op jit(solution)/shard_map/ppermute | solution.py:88
  99.9 35.2 %collective-permute-start.10 = (bf16[32,6144]{1,0:T(8,128)(2,1)}, bf16[32,6144]{1,0:T(8,128)(2,1)S(1)}, u32[]{:S(2)}, u32[]{:S(2)}) collective-permute-start(bf16[32,6144]{1,0:T(8,128)(2,1)} %get-tuple-element.86), channel_id=1, source_target_pairs={{0,2},{1,3},{2,4},{3,5},{4,6},{5,7},{6,0},{7,1},{8,10},{9,11},{10,... | collective-permute-start | bytes 1179656 | tf_op jit(solution)/shard_map/ppermute | solution.py:88
  107.9 27.2 %copy-start.8 = (bf16[32,6144]{1,0:T(8,128)(2,1)}, bf16[32,6144]{1,0:T(8,128)(2,1)S(1)}, u32[]{:S(2)}) copy-start(bf16[32,6144]{1,0:T(8,128)(2,1)S(1)} %collective-permute-done.12.refs_2_) | copy-start | bytes 1179652
  135.1 0.7 copy-start.9
  135.8 0.7 copy-start.10
  138.9 27.8 %collective-permute-start.17 = (bf16[96,6144]{1,0:T(8,128)(2,1)}, bf16[96,6144]{1,0:T(8,128)(2,1)}, u32[]{:S(2)}, u32[]{:S(2)}) collective-permute-start(bf16[96,6144]{1,0:T(8,128)(2,1)} %stack.1.refs_2_), channel_id=1, source_target_pairs={{0,1},{1,0},{2,3},{3,2},{4,5},{5,4},{6,7},{7,6},{8,9},{9,8},{10,11... | collective-permute-start | bytes 3538952 | tf_op jit(solution)/shard_map/ppermute | solution.py:88
  138.9 61.0 %collective-permute-start.15 = (bf16[96,6144]{1,0:T(8,128)(2,1)}, bf16[96,6144]{1,0:T(8,128)(2,1)}, u32[]{:S(2)}, u32[]{:S(2)}) collective-permute-start(bf16[96,6144]{1,0:T(8,128)(2,1)} %stack.1.refs_2_), channel_id=1, source_target_pairs={{0,24},{1,25},{2,26},{3,27},{4,28},{5,29},{6,30},{7,31},{8,16},{9,... | collective-permute-start | bytes 3538952 | tf_op jit(solution)/shard_map/ppermute | solution.py:88
  140.3 59.6 %collective-permute-start.14 = (bf16[96,6144]{1,0:T(8,128)(2,1)}, bf16[96,6144]{1,0:T(8,128)(2,1)}, u32[]{:S(2)}, u32[]{:S(2)}) collective-permute-start(bf16[96,6144]{1,0:T(8,128)(2,1)} %stack.1.refs_2_), channel_id=1, source_target_pairs={{0,16},{1,17},{2,18},{3,19},{4,20},{5,21},{6,22},{7,23},{8,24},{9,... | collective-permute-start | bytes 3538952 | tf_op jit(solution)/shard_map/ppermute | solution.py:88
  141.8 58.1 %collective-permute-start.13 = (bf16[96,6144]{1,0:T(8,128)(2,1)}, bf16[96,6144]{1,0:T(8,128)(2,1)}, u32[]{:S(2)}, u32[]{:S(2)}) collective-permute-start(bf16[96,6144]{1,0:T(8,128)(2,1)} %stack.1.refs_2_), channel_id=1, source_target_pairs={{0,8},{1,9},{2,10},{3,11},{4,12},{5,13},{6,14},{7,15},{8,0},{9,1},... | collective-permute-start | bytes 3538952 | tf_op jit(solution)/shard_map/ppermute | solution.py:88
  142.4 58.5 %collective-permute-start.6 = (bf16[128,6144]{1,0:T(8,128)(2,1)}, bf16[128,6144]{1,0:T(8,128)(2,1)S(1)}, u32[]{:S(2)}, u32[]{:S(2)}) collective-permute-start(bf16[128,6144]{1,0:T(8,128)(2,1)} %get-tuple-element.84.refs_0_), channel_id=1, source_target_pairs={{0,1},{1,0},{2,3},{3,2},{4,5},{5,4},{6,7},{7,6},{8,9},{9,8},{10,11... | collective-permute-start | bytes 4718600 | tf_op jit(solution)/shard_map/ppermute | solution.py:88
  199.9 3.2 collective-permute-start.18
  200.4 4.4 %collective-permute-start.19 = (bf16[96,6144]{1,0:T(8,128)(2,1)}, bf16[96,6144]{1,0:T(8,128)(2,1)S(1)}, u32[]{:S(2)}, u32[]{:S(2)}) collective-permute-start(bf16[96,6144]{1,0:T(8,128)(2,1)} %collective-permute-done.14.refs_4_), channel_id=1, source_target_pairs={{0,1},{1,0},{2,3},{3,2},{4,5},{5,4},{6,7},{7,6},{8,9},{9,8},{10,11... | collective-permute-start | bytes 3538952 | tf_op jit(solution)/shard_map/ppermute | solution.py:88
  200.5 6.0 %collective-permute-start.20 = (bf16[96,6144]{1,0:T(8,128)(2,1)}, bf16[96,6144]{1,0:T(8,128)(2,1)S(1)}, u32[]{:S(2)}, u32[]{:S(2)}) collective-permute-start(bf16[96,6144]{1,0:T(8,128)(2,1)} %collective-permute-done.15.refs_5_), channel_id=1, source_target_pairs={{0,1},{1,0},{2,3},{3,2},{4,5},{5,4},{6,7},{7,6},{8,9},{9,8},{10,11... | collective-permute-start | bytes 3538952 | tf_op jit(solution)/shard_map/ppermute | solution.py:88
  201.0 5.5 %copy-start.2 = (bf16[128,6144]{1,0:T(8,128)(2,1)}, bf16[128,6144]{1,0:T(8,128)(2,1)S(1)}, u32[]{:S(2)}) copy-start(bf16[128,6144]{1,0:T(8,128)(2,1)S(1)} %collective-permute-done.6.refs_1_) | copy-start | bytes 4718596
  203.1 3.4 copy-start.4
  204.8 1.7 copy-start.5
  206.5 1.0 copy-start.6
  329.9 1.6 collective-permute-start.21
  332.4 5.4 %collective-permute-start.24 = (f32[16,1024]{1,0:T(8,128)S(1)}, f32[16,1024]{1,0:T(8,128)S(1)}, u32[]{:S(2)}, u32[]{:S(2)}) collective-permute-start(f32[16,1024]{1,0:T(8,128)S(1)} %add.21), channel_id=1, source_target_pairs={{0,24},{1,25},{2,26},{3,27},{4,28},{5,29},{6,30},{7,31},{8,16},{9,... | collective-permute-start | bytes 196616 | tf_op jit(solution)/shard_map/ppermute | solution.py:88
  333.8 5.2 %collective-permute-start.23 = (f32[16,1024]{1,0:T(8,128)S(1)}, f32[16,1024]{1,0:T(8,128)S(1)}, u32[]{:S(2)}, u32[]{:S(2)}) collective-permute-start(f32[16,1024]{1,0:T(8,128)S(1)} %add.21), channel_id=1, source_target_pairs={{0,16},{1,17},{2,18},{3,19},{4,20},{5,21},{6,22},{7,23},{8,24},{9,... | collective-permute-start | bytes 196616 | tf_op jit(solution)/shard_map/ppermute | solution.py:88
  335.3 4.3 %collective-permute-start.22 = (f32[16,1024]{1,0:T(8,128)S(1)}, f32[16,1024]{1,0:T(8,128)S(1)}, u32[]{:S(2)}, u32[]{:S(2)}) collective-permute-start(f32[16,1024]{1,0:T(8,128)S(1)} %add.21), channel_id=1, source_target_pairs={{0,8},{1,9},{2,10},{3,11},{4,12},{5,13},{6,14},{7,15},{8,0},{9,1},... | collective-permute-start | bytes 196616 | tf_op jit(solution)/shard_map/ppermute | solution.py:88
  339.6 28.3 %collective-permute-start.27 = (f32[16,1024]{1,0:T(8,128)S(1)}, f32[16,1024]{1,0:T(8,128)S(1)}, u32[]{:S(2)}, u32[]{:S(2)}) collective-permute-start(f32[16,1024]{1,0:T(8,128)S(1)} %add_add_fusion.1), channel_id=1, source_target_pairs={{0,6},{1,7},{2,0},{3,1},{4,2},{5,3},{6,4},{7,5},{8,14},{9,15},{10,... | collective-permute-start | bytes 196616 | tf_op jit(solution)/shard_map/ppermute | solution.py:88
  339.6 28.2 %collective-permute-start.26 = (f32[16,1024]{1,0:T(8,128)S(1)}, f32[16,1024]{1,0:T(8,128)S(1)}, u32[]{:S(2)}, u32[]{:S(2)}) collective-permute-start(f32[16,1024]{1,0:T(8,128)S(1)} %add_add_fusion.1), channel_id=1, source_target_pairs={{0,4},{1,5},{2,6},{3,7},{4,0},{5,1},{6,2},{7,3},{8,12},{9,13},{10,... | collective-permute-start | bytes 196616 | tf_op jit(solution)/shard_map/ppermute | solution.py:88
  339.7 28.1 %collective-permute-start.25 = (f32[16,1024]{1,0:T(8,128)S(1)}, f32[16,1024]{1,0:T(8,128)S(1)}, u32[]{:S(2)}, u32[]{:S(2)}) collective-permute-start(f32[16,1024]{1,0:T(8,128)S(1)} %add_add_fusion.1), channel_id=1, source_target_pairs={{0,2},{1,3},{2,4},{3,5},{4,6},{5,7},{6,0},{7,1},{8,10},{9,11},{10,... | collective-permute-start | bytes 196616 | tf_op jit(solution)/shard_map/ppermute | solution.py:88
